TPU v7x, 256 devices: a whole 4x4x8 slice. The times are simulated.
256 devices in a mesh: pool: 128 (over x, z, y), pd: 2 (over core).
Axes of the slice: x: 4, y: 4, z: 8, core: 2. Of those that a mesh axis runs over, the one named last changes fastest.
Arguments:
- q_latent: bfloat16 [8192, 128, 512], P('pool', 'pd')
- q_rope: bfloat16 [8192, 8192], P('pool', 'pd'), may hold values from -6 to 6
- new_latent: bfloat16 [8192, 576], P('pool'), may hold values from -6 to 6
- pool_pages: bfloat16 [2048, 64, 576], P('pool')
- page_owner: int32 [128, 24], P('pool'), may hold values from 0 to 127, as said below
- page_slot: int32 [128, 24], P('pool'), may hold values from 0 to 15, as said below
- prefix_len: int32 [128], P('pool'), may hold values from 1152 to 1536, as said below
- partner: int32 [128], P('pool'), may hold values from 0 to 127, as said below
- dest_slot: int32 [128], P('pool'), may hold values from 0 to 7
- decode_cache: bfloat16 [1024, 64, 576], P('pool'), may hold values from -6 to 6
Outputs:
- context: bfloat16 [8192, 128, 512], P('pool', 'pd')
- decode_out: bfloat16 [1024, 64, 576], P('pool')
Inputs may be any that keep to these rules, and one draw needn't show every extreme that they name: `page_owner`: the 24 owners of one stretch are all different; page 0 of every stretch is the same page, at one owner and slot drawn from the seed. `page_slot`: slots within an owner. `prefix_len`: some stretch has the longest prefix. Each decode device is the partner of exactly one stretch; some stretch c and stretch (c + 64) mod 128 are each other's partners.
All inputs are finite; a program needn't handle non-finite values.
Results may differ from a plain program's by a relative error of at most 0.006.
Values may be sent and summed in bfloat16 or wider, within the bound.
No kernel may reach another device: no remote copies, remote signals or barrier semaphores. Data moves between devices by JAX's collectives and lax.ppermute only.
A program may use at most 128 MiB of HBM per device.

v0:
```python
import jax
import jax.numpy as jnp
from jax import lax
from jax.sharding import PartitionSpec as P

score_scale = 192.0 ** (-0.5)


def absorb(carry, queries, keys, visible, latent):
    best, total, summed = carry
    scores = (
        jnp.einsum("qd,kd->qk", queries, keys, preferred_element_type=jnp.float32) * score_scale
    )
    masked = jnp.where(visible, scores, jnp.float32(-1e30))
    top = jnp.maximum(best, jnp.max(masked, axis=1))
    shrink = jnp.exp(best - top)
    weight = jnp.where(visible, jnp.exp(scores - top[:, None]), jnp.float32(0.0))
    total = total * shrink + jnp.sum(weight, axis=1)
    summed = summed * shrink[:, None] + jnp.dot(
        weight.astype(jnp.bfloat16), keys[:, :latent], preferred_element_type=jnp.float32
    )
    return (top, total, summed)


def body(
    q_latent,
    q_rope,
    new_latent,
    pool_pages,
    page_owner,
    page_slot,
    prefix_len,
    partner,
    dest_slot,
    decode_cache,
):
    stretch, heads, latent = q_latent.shape
    rope = q_rope.shape[1] // heads
    slots, page, width = pool_pages.shape
    most = page_owner.shape[1]
    owners = lax.axis_size("pool")
    length = prefix_len[0]
    needed = (length + page - 1) // page
    listed = jnp.arange(most, dtype=jnp.int32) < needed
    match = (page_owner[0][:, None] == jnp.arange(owners, dtype=jnp.int32)[None, :]) & listed[
        :, None
    ]
    wanted = jnp.sum(jnp.where(match, page_slot[0][:, None] + 1, 0), axis=0) - 1
    requests = wanted[:, None]
    asked = lax.all_to_all(requests, "pool", split_axis=0, concat_axis=0, tiled=True)
    usable = asked >= 0
    picked = jnp.take(pool_pages, jnp.clip(asked, 0, slots - 1), axis=0)
    picked = jnp.where(usable[:, :, None, None], picked, jnp.zeros((), pool_pages.dtype))
    replies = lax.all_to_all(picked, "pool", split_axis=0, concat_axis=0, tiled=True)
    fetched = jnp.take(replies[:, 0], page_owner[0], axis=0)
    queries = jnp.concatenate([q_latent, q_rope.reshape(stretch, heads, rope)], axis=2).reshape(
        stretch * heads, width
    )
    rows = stretch * heads
    group = 1
    for trial in range(1, most + 1):
        if most % trial == 0 and trial * page <= max(512, page):
            group = trial
    span = group * page
    blocks = fetched.reshape(most // group, span, width)
    starts = jnp.arange(most // group, dtype=jnp.int32) * span

    def step(carry, item):
        keys, first = item
        visible = (first + jnp.arange(span, dtype=jnp.int32) < length)[None, :]
        return (absorb(carry, queries, keys, visible, latent), None)

    start_carry = (
        jnp.full((rows,), -1e30, jnp.float32),
        jnp.zeros((rows,), jnp.float32),
        jnp.zeros((rows, latent), jnp.float32),
    )
    carry, unused = lax.scan(step, start_carry, (blocks, starts))
    token_of = jnp.arange(rows, dtype=jnp.int32) // heads
    causal = jnp.arange(stretch, dtype=jnp.int32)[None, :] <= token_of[:, None]
    best, total, summed = absorb(carry, queries, new_latent, causal, latent)
    context = (summed / total[:, None]).astype(jnp.bfloat16).reshape(stretch, heads, latent)
    target_hit = jnp.arange(owners, dtype=jnp.int32) == partner[0]
    outgoing = jnp.where(
        target_hit[:, None, None], new_latent[None], jnp.zeros((), new_latent.dtype)
    )
    incoming = lax.all_to_all(outgoing, "pool", split_axis=0, concat_axis=0, tiled=True)
    arrived = jnp.sum(incoming.astype(jnp.float32), axis=0).astype(jnp.bfloat16)
    slot_hit = jnp.arange(decode_cache.shape[0], dtype=jnp.int32) == dest_slot[0]
    decode_out = jnp.where(slot_hit[:, None, None], arrived[None], decode_cache)
    return (context, decode_out)


def solution(mesh):
    placed = (
        P("pool", "pd", None),
        P("pool", "pd"),
        P("pool", None),
        P("pool", None, None),
        P("pool", None),
        P("pool", None),
        P("pool"),
        P("pool"),
        P("pool"),
        P("pool", None, None),
    )
    return jax.shard_map(
        body,
        mesh=mesh,
        in_specs=placed,
        out_specs=(P("pool", "pd", None), P("pool", None, None)),
        check_vma=False,
    )
```

profile of v0, /device:TPU:1, one launch (start us, length us, event | category | flops | bytes accessed | tf_op | source)
XLA Modules:
  0.0 589.7 jit_solution(9920183369352069036)
XLA Ops:
  1.4 0.7 add_bitcast_fusion.1
  2.1 0.7 select_reduce_fusion.2
  2.8 0.7 copy.15
  3.6 16.3 %all-to-all-start = ((s32[128,1,1]{2,1,0:T(1,128)}), s32[128,1,1]{2,1,0:T(1,128)S(1)}, u32[]{:S(2)}, u32[]{:S(2)}) async-start(s32[128,1,1]{2,1,0:T(1,128)} %copy.15), calls=%async_computation | async-start | bytes 131072 | tf_op jit(solution)/shard_map/all_to_all | solution.py:50
  20.6 5.7 broadcast_select_fusion
  26.3 4.1 all-to-all-done
  30.4 9.8 %all-to-all-start.2 = ((bf16[128,64,576]{2,1,0:T(8,128)(2,1)}), bf16[128,64,576]{2,1,0:T(8,128)(2,1)}, u32[]{:S(2)}, u32[]{:S(2)}) async-start(bf16[128,64,576]{2,1,0:T(8,128)(2,1)} %broadcast_select_fusion), calls=%async_computation.2 | async-start | bytes 20971520 | tf_op jit(solution)/shard_map/all_to_all | solution.py:87
  40.2 4.6 and_reduce_fusion
  44.8 2.4 reduce.6
  47.2 7.4 %gather_fusion = bf16[128,64,576]{2,1,0:T(8,128)(2,1)} fusion(bf16[16,64,576]{2,1,0:T(8,128)(2,1)S(1)} %copy-done, s32[1024]{0:T(1024)S(1)} %pad_clamp_fusion.1), kind=kCustom, calls=%fused_computation | custom fusion | bytes 18874880 | tf_op jit(solution)/shard_map/jit(_take)/gather | solution.py:52
  54.6 10.6 %fusion.12 = bf16[128,1,64,576]{3,2,1,0:T(8,128)(2,1)} fusion(bf16[128,64,576]{2,1,0:T(8,128)(2,1)} %gather_fusion, pred[128]{0:T(512)(128)(4,1)S(1)} %get-tuple-element.96, pred[128]{0:T(512)(128)(4,1)S(1)} %get-tuple-element.100), kind=kLoop, calls=%fused_computation.22 | loop fusion | flops 9437184 | bytes 18874624 | tf_op jit(solution)/shard_map/jit(_where)/select_n | solution.py:53
  65.3 201.5 %all-to-all-done.2 = bf16[128,64,576]{2,1,0:T(8,128)(2,1)} async-done(((bf16[128,64,576]{2,1,0:T(8,128)(2,1)}), bf16[128,64,576]{2,1,0:T(8,128)(2,1)}, u32[]{:S(2)}, u32[]{:S(2)}) %all-to-all-start.2) | async-done | bytes 9437216 | tf_op jit(solution)/shard_map/all_to_all | solution.py:87
  266.8 12.7 %all-to-all-start.1 = ((bf16[128,1,64,576]{3,2,1,0:T(8,128)(2,1)}), bf16[128,1,64,576]{3,2,1,0:T(8,128)(2,1)}, u32[]{:S(2)}, u32[]{:S(2)}) async-start(bf16[128,1,64,576]{3,2,1,0:T(8,128)(2,1)} %fusion.12), calls=%async_computation.1 | async-start | bytes 20971520 | tf_op jit(solution)/shard_map/all_to_all | solution.py:54
  279.5 0.5 broadcast.260
  280.0 0.7 reduce.11
  280.7 0.1 squeeze.28
  280.8 0.1 broadcast_in_dim.137
  280.8 0.1 broadcast_in_dim.138
  280.9 1.1 concatenate.9
  282.9 5.1 select_reduce_fusion.1
  288.0 2.9 pad_maximum_fusion
  291.0 5.6 reduce_sum.41
  296.6 1.0 broadcast_select_fusion.1
  297.6 208.2 %all-to-all-done.1 = bf16[128,1,64,576]{3,2,1,0:T(8,128)(2,1)} async-done(((bf16[128,1,64,576]{3,2,1,0:T(8,128)(2,1)}), bf16[128,1,64,576]{3,2,1,0:T(8,128)(2,1)}, u32[]{:S(2)}, u32[]{:S(2)}) %all-to-all-start.1) | async-done | bytes 9437216 | tf_op jit(solution)/shard_map/all_to_all | solution.py:54
  505.8 6.1 %gather_fusion.1 = bf16[24,64,576]{2,1,0:T(8,128)(2,1)} fusion(bf16[128,64,576]{2,1,0:T(8,128)(2,1)} %bitcast.5, s32[1024]{0:T(1024)S(1)} %pad_clamp_fusion), kind=kCustom, calls=%fused_computation.1 | custom fusion | bytes 3539040 | tf_op jit(solution)/shard_map/jit(_take)/gather | solution.py:55
  511.9 1.9 bitcast_select_fusion.1
  513.8 68.3 %while.15 = (s32[]{:T(128)}, f32[4096]{0:T(1024)S(1)}, f32[4096]{0:T(1024)S(1)}, f32[4096,512]{1,0:T(8,128)}, s32[3]{0:T(128)S(1)}, /*index=5*/s32[]{:T(128)}, b...) while((s32[]{:T(128)}, f32[4096]{0:T(1024)S(1)}, ...), condition=%wide.region_4.5_spmd.clone, body=%wide.region_1.4_spmd.clone.sunk | while | flops 4592784384 | bytes 82774184 | solution.py:78
  513.8 0.6 dynamic_slice.14
  514.4 1.3 add_compare_fusion.2
  515.7 0.1 dynamic-slice_bitcast_fusion.2
  515.8 8.4 %select_reduce_fusion.4 = (f32[4096]{0:T(1024)S(1)}, f32[512,4096]{1,0:T(8,128)}) fusion(pred[512]{0:T(512)(128)(4,1)S(1)} %add_compare_fusion.2, bf16[512,576]{1,0:T(8,128)(2,1)S(1)} %dynamic-slice_bitcast_fusion.2, bf16[4096,576]{1,0:T(8,128)(2,1)} %get-tuple-element.187), kind=kOutput, calls=%fused_computation.5.clone.1 | convolution fusion | flops 2422206464 | bytes 13713920 | tf_op jit(solution)/shard_map/while/body/eval_jaxpr/qd,kd->qk/dot_general | solution.py:12
  524.2 5.0 fusion.40
  529.2 0.8 copy-done.2
  530.0 5.1 fusion.42
  535.2 0.6 dynamic_slice.14
  535.7 1.3 add_compare_fusion.2
  537.1 8.4 %select_reduce_fusion.4 = (f32[4096]{0:T(1024)S(1)}, f32[512,4096]{1,0:T(8,128)}) fusion(pred[512]{0:T(512)(128)(4,1)S(1)} %add_compare_fusion.2, bf16[512,576]{1,0:T(8,128)(2,1)S(1)} %dynamic-slice_bitcast_fusion.2, bf16[4096,576]{1,0:T(8,128)(2,1)} %get-tuple-element.187), kind=kOutput, calls=%fused_computation.5.clone.1 | convolution fusion | flops 2422206464 | bytes 13713920 | tf_op jit(solution)/shard_map/while/body/eval_jaxpr/qd,kd->qk/dot_general | solution.py:12
  545.5 5.0 fusion.40
  550.5 0.8 copy-done.2
  551.3 7.3 %fusion.42 = f32[4096,512]{1,0:T(8,128)} fusion(f32[4096,512]{1,0:T(8,128)} %get-tuple-element.173, f32[512,4096]{1,0:T(8,128)S(1)} %copy-done.2, f32[4096]{0:T(1024)S(1)} %get-tuple-element.159, f32[4096]{0:T(1024)S(1)} %select_maximum_fusion.2, pred[512]{0:T(512)(128)(4,1)S(1)} %add_compare_fusion.2, pred[]{:T(512)S(6)} %compare.9, ...), kind=kOutput, calls=%fused_computation.3.clone.1 | convolution fusion | flops 2162163712 | bytes 25723392 | tf_op jit(solution)/shard_map/while/body/eval_jaxpr/dot_general | solution.py:19
  558.7 0.6 dynamic_slice.14
  559.2 1.3 add_compare_fusion.2
  560.6 8.4 %select_reduce_fusion.4 = (f32[4096]{0:T(1024)S(1)}, f32[512,4096]{1,0:T(8,128)}) fusion(pred[512]{0:T(512)(128)(4,1)S(1)} %add_compare_fusion.2, bf16[512,576]{1,0:T(8,128)(2,1)S(1)} %dynamic-slice_bitcast_fusion.2, bf16[4096,576]{1,0:T(8,128)(2,1)} %get-tuple-element.187), kind=kOutput, calls=%fused_computation.5.clone.1 | convolution fusion | flops 2422206464 | bytes 13713920 | tf_op jit(solution)/shard_map/while/body/eval_jaxpr/qd,kd->qk/dot_general | solution.py:12
  569.0 5.0 fusion.40
  574.0 0.8 copy-done.2
  574.8 7.3 %fusion.42 = f32[4096,512]{1,0:T(8,128)} fusion(f32[4096,512]{1,0:T(8,128)} %get-tuple-element.173, f32[512,4096]{1,0:T(8,128)S(1)} %copy-done.2, f32[4096]{0:T(1024)S(1)} %get-tuple-element.159, f32[4096]{0:T(1024)S(1)} %select_maximum_fusion.2, pred[512]{0:T(512)(128)(4,1)S(1)} %add_compare_fusion.2, pred[]{:T(512)S(6)} %compare.9, ...), kind=kOutput, calls=%fused_computation.3.clone.1 | convolution fusion | flops 2162163712 | bytes 25723392 | tf_op jit(solution)/shard_map/while/body/eval_jaxpr/dot_general | solution.py:19
  582.2 1.5 fusion.13
  583.7 6.1 %divide_convert_fusion = bf16[4096,512]{1,0:T(8,128)(2,1)} fusion(f32[4096,512]{1,0:T(8,128)} %get-tuple-element.46, f32[4096]{0:T(1024)S(1)} %get-tuple-element.94, f32[4096]{0:T(1024)S(1)} %get-tuple-element.95, f32[4096,64]{0,1:T(8,128)} %get-tuple-element.102, f32[4096]{0:T(1024)S(1)} %max.10, s32[4096]{0:T(1024)S(1)} %add_select_fusion, ...), kind=kOutput, calls=%fused_computation.24 | convolution fusion | flops 277872640 | bytes 13762560 | tf_op jit(solution)/shard_map/dot_general | solution.py:19
  (43 shorter events, 0.3 us)
Async XLA Ops:
  0.6 46.6 %copy-start = (bf16[16,64,576]{2,1,0:T(8,128)(2,1)S(1)}, bf16[16,64,576]{2,1,0:T(8,128)(2,1)}, u32[]{:S(2)}) copy-start(bf16[16,64,576]{2,1,0:T(8,128)(2,1)} %param.15) | copy-start | bytes 3538948
  3.6 26.8 %all-to-all-start = ((s32[128,1,1]{2,1,0:T(1,128)}), s32[128,1,1]{2,1,0:T(1,128)S(1)}, u32[]{:S(2)}, u32[]{:S(2)}) async-start(s32[128,1,1]{2,1,0:T(1,128)} %copy.15), calls=%async_computation | async-start | bytes 131072 | tf_op jit(solution)/shard_map/all_to_all | solution.py:50
  30.4 236.3 %all-to-all-start.2 = ((bf16[128,64,576]{2,1,0:T(8,128)(2,1)}), bf16[128,64,576]{2,1,0:T(8,128)(2,1)}, u32[]{:S(2)}, u32[]{:S(2)}) async-start(bf16[128,64,576]{2,1,0:T(8,128)(2,1)} %broadcast_select_fusion), calls=%async_computation.2 | async-start | bytes 20971520 | tf_op jit(solution)/shard_map/all_to_all | solution.py:87
  65.3 214.7 %copy-start.7 = (s32[1,24]{1,0:T(1,128)S(1)}, s32[1,24]{1,0:T(1,128)}, u32[]{:S(2)}) copy-start(s32[1,24]{1,0:T(1,128)} %param.16) | copy-start | bytes 292
  65.3 215.7 %copy-start.5 = (bf16[64,4096]{1,0:T(8,128)(2,1)S(1)}, bf16[64,4096]{1,0:T(8,128)(2,1)}, u32[]{:S(2)}) copy-start(bf16[64,4096]{1,0:T(8,128)(2,1)} %param.13) | copy-start | bytes 1572868
  65.3 217.7 %copy-start.6 = (bf16[64,576]{1,0:T(8,128)(2,1)S(1)}, bf16[64,576]{1,0:T(8,128)(2,1)}, u32[]{:S(2)}) copy-start(bf16[64,576]{1,0:T(8,128)(2,1)} %param.14) | copy-start | bytes 221188
  266.8 239.0 %all-to-all-start.1 = ((bf16[128,1,64,576]{3,2,1,0:T(8,128)(2,1)}), bf16[128,1,64,576]{3,2,1,0:T(8,128)(2,1)}, u32[]{:S(2)}, u32[]{:S(2)}) async-start(bf16[128,1,64,576]{3,2,1,0:T(8,128)(2,1)} %fusion.12), calls=%async_computation.1 | async-start | bytes 20971520 | tf_op jit(solution)/shard_map/all_to_all | solution.py:54
  282.1 6.0 %copy-start.3 = (bf16[64,64,512]{2,1,0:T(8,128)(2,1)S(1)}, bf16[64,64,512]{2,1,0:T(8,128)(2,1)}, u32[]{:S(2)}) copy-start(bf16[64,64,512]{2,1,0:T(8,128)(2,1)} %param.12) | copy-start | bytes 12582916
  288.0 8.6 %copy-start.4 = (bf16[8,64,576]{2,1,0:T(8,128)(2,1)S(1)}, bf16[8,64,576]{2,1,0:T(8,128)(2,1)}, u32[]{:S(2)}) copy-start(bf16[8,64,576]{2,1,0:T(8,128)(2,1)} %param.21) | copy-start | bytes 1769476
  524.2 5.8 copy-start.2
  545.5 5.8 copy-start.2
  569.0 5.8 copy-start.2
  583.7 6.1 %copy-start.1 = (bf16[16,64,576]{2,1,0:T(8,128)(2,1)S(1)}, bf16[16,64,576]{2,1,0:T(8,128)(2,1)}, u32[]{:S(2)}) copy-start(bf16[16,64,576]{2,1,0:T(8,128)(2,1)} %param.15) | copy-start | bytes 3538948
where the time goes:
time: 595 us; the launch traced here: 590 us
  waiting for transfers between devices  414 us (70%)
  other arithmetic  57.2 us (10%)
  matrix products  56.1 us (9%)
  starting transfers between devices  38.8 us (7%)
  local copies, waits for them, and re-layouts  20.7 us (3%)
    all_to_all x1, waiting for transfers between devices, body(): lax.all_to_all(picked, 'pool', split_axis=0, concat_axis=0, tiled=True)  208 us
    all_to_all x1, waiting for transfers between devices, body(): lax.all_to_all(outgoing, 'pool', split_axis=0, concat_axis=0, tiled=True)  202 us
    dot_general x4, matrix products, absorb(): jnp.einsum('qd,kd->qk', queries, keys, preferred_element_type=jnp.float32)  30.2 us
    dot_general x4, matrix products, absorb(): jnp.dot(weight.astype(jnp.bfloat16), keys[:, :latent], preferred_element_...  25.8 us
    all_to_all x1, starting transfers between devices, body(): lax.all_to_all(requests, 'pool', split_axis=0, concat_axis=0, tiled=True)  16.3 us
    reduce_sum x4, other arithmetic, absorb(): total = total * shrink + jnp.sum(weight, axis=1)  16.3 us
    all_to_all x1, starting transfers between devices, body(): lax.all_to_all(picked, 'pool', split_axis=0, concat_axis=0, tiled=True)  12.7 us
  transfers between devices with their start and end apart: 3, of which 3 were waited for; matrix products, arithmetic and copies ran while one was open for 8% of the time, Pallas kernels for 0%

commit v1 on v0

v1 whole, which is shorter than its diff:
```python
import functools

import jax
import jax.numpy as jnp
from jax import lax
from jax.experimental import pallas as pl
from jax.experimental.pallas import tpu as pltpu
from jax.sharding import PartitionSpec as P

score_scale = 192.0 ** (-0.5)
log2_e = 1.4426950408889634
hidden = -1e30
lanes = 128
f32 = jnp.float32
bf16 = jnp.bfloat16


def iota(shape, axis):
    return lax.broadcasted_iota(jnp.int32, shape, axis)


def picks(condition):
    return jnp.where(condition, jnp.float32(1.0), jnp.float32(0.0)).astype(bf16)


def mm(a, b):
    return lax.dot_general(a, b, (((1,), (0,)), ((), ())), preferred_element_type=f32)


def mm_first(a, b):
    return lax.dot_general(a, b, (((0,), (0,)), ((), ())), preferred_element_type=f32)


def mm_last(a, b):
    return lax.dot_general(a, b, (((1,), (1,)), ((), ())), preferred_element_type=f32)


def spread_kernel(half_ref, pages_ref, new_ref, meta_ref, out_ref):
    slots, rows, width = pages_ref.shape
    held = 24
    pages = pages_ref[...].reshape(slots * rows, width)
    fresh = new_ref[...]
    latent = 4 * lanes
    total = rows * held
    out_row = iota((total, 1), 0)
    out_r = out_row // held
    out_k = out_row % held
    in_row = iota((total, slots * rows), 1)
    in_r = in_row % rows
    in_s = in_row // rows
    same = in_r == out_r
    take_latent = picks(same & (in_s == out_k))
    take_rope = picks(same & (in_s // 8 == out_k - 17))
    new_same = iota((total, rows), 1) == out_r
    take_new = picks(new_same & (out_k == 16))
    take_new_rope = picks(new_same & (out_k == 19))
    src = iota((64, latent), 0)
    dst = iota((64, latent), 1)
    tile = picks((src // 16 == dst // lanes) & (src % 16 == dst % 16))
    group = (iota((slots * rows, latent), 1) % lanes) // 16
    slot = iota((slots * rows, latent), 0) // rows
    rope = mm(pages[:, latent:], tile)
    rope = jnp.where(group == slot % 8, rope, 0.0).astype(bf16)
    new_rope = mm(fresh[:, latent:], tile).astype(bf16)
    result = mm(take_latent, pages[:, :latent]) + mm(take_rope, rope)
    result += mm(take_new, fresh[:, :latent]) + mm(take_new_rope, new_rope)
    meta = meta_ref[...].astype(f32)
    for quarter in range(4):
        part = result[:, quarter * lanes : (quarter + 1) * lanes]
        part = jnp.where(out_k == 20, meta, part)
        out_ref[quarter * rows : (quarter + 1) * rows] = part.reshape(rows, held, lanes).astype(bf16)


def spread(half, pages, fresh, meta):
    slots, page, width = pages.shape
    rows = page // 2
    return pl.pallas_call(
        spread_kernel,
        grid_spec=pltpu.PrefetchScalarGridSpec(
            num_scalar_prefetch=1,
            grid=(1,),
            in_specs=[
                pl.BlockSpec((slots, rows, width), lambda i, half: (0, half[0], 0)),
                pl.BlockSpec((rows, width), lambda i, half: (half[0], 0)),
                pl.BlockSpec((1, lanes), lambda i, half: (0, 0)),
            ],
            out_specs=pl.BlockSpec((4 * rows, 24, lanes), lambda i, half: (0, 0, 0)),
        ),
        out_shape=jax.ShapeDtypeStruct((4 * rows, 24, lanes), bf16),
        compiler_params=pltpu.CompilerParams(vmem_limit_bytes=40 * 1024 * 1024),
        cost_estimate=pl.CostEstimate(flops=10**9, bytes_accessed=1_500_000, transcendentals=0),
    )(half, pages, fresh, meta)


def collect_kernel(block, all_ref, mine_ref, out_ref, table_ref):
    step = pl.program_id(0)
    owners = all_ref.shape[0]
    pages = 24

    @pl.when(step == 0)
    def build():
        src = iota((lanes, lanes), 0)
        dst = iota((lanes, lanes), 1)
        tile = picks(src % 16 == dst % 16)
        group = iota((8, lanes), 1) // 16 == iota((8, lanes), 0)
        chunk = 32
        for first in range(0, owners, chunk):
            held = all_ref[first : first + chunk].astype(f32)
            table_ref[first * 16 : (first + chunk) * 16, :lanes] = (
                held[:, :16].reshape(chunk * 16, lanes).astype(bf16)
            )
            pieces = [
                jnp.where(group[None], held[:, 17 + k : 18 + k], 0.0) for k in range(2)
            ]
            rope = jnp.concatenate(pieces, axis=1).reshape(chunk * 16, lanes).astype(bf16)
            table_ref[first * 16 : (first + chunk) * 16, lanes:] = mm(rope, tile).astype(bf16)

    rows = block * pages
    row = iota((rows, 1), 0)
    stretch = row // pages
    place = row % pages
    meta = mine_ref[:, 16:24].astype(f32)[:, 4, :].astype(bf16)
    expand = picks(iota((rows, block), 1) == stretch)
    spread_meta = mm(expand, meta)
    lane = iota((rows, lanes), 1)
    weight = jnp.where(lane == place, 16.0, jnp.where(lane == place + 32, 1.0, 0.0))
    index = jnp.sum(spread_meta * weight, axis=1, keepdims=True).astype(jnp.int32)
    wanted = picks(iota((rows, owners * 16), 1) == index)
    found = mm(wanted, table_ref[...])
    latent = found[:, :lanes].reshape(block, pages, lanes)
    rope = jnp.where(lane // 16 == place % 8, found[:, lanes:], 0.0).astype(bf16)
    last = iota((block * 8, rows), 0)
    other = iota((block * 8, rows), 1)
    gather_rope = picks(
        (last // 8 == other // pages) & (last % 8 - 1 == (other % pages) // 8)
    )
    tail = mm(gather_rope, rope)
    held = all_ref[:, 16:24].astype(f32)
    partner = held[:, 4, 64:65].astype(jnp.int32)
    target = iota((owners, block * 8), 1)
    arrives = partner == target // 8 + step * block
    tail += mm_first(picks(arrives & (target % 8 == 0)), held[:, 0, :].astype(bf16))
    tail += mm_first(picks(arrives & (target % 8 == 4)), held[:, 3, :].astype(bf16))
    tail = tail.reshape(block, 8, lanes)
    out_ref[...] = jnp.concatenate([latent, tail], axis=1).astype(bf16)


def collect(held):
    owners = held.shape[0]
    block = 16
    return pl.pallas_call(
        functools.partial(collect_kernel, block),
        grid=(owners // block,),
        in_specs=[
            pl.BlockSpec(held.shape, lambda i: (0, 0, 0)),
            pl.BlockSpec((block, 24, lanes), lambda i: (i, 0, 0)),
        ],
        out_specs=pl.BlockSpec((block, 32, lanes), lambda i: (i, 0, 0)),
        out_shape=jax.ShapeDtypeStruct((owners, 32, lanes), bf16),
        scratch_shapes=[pltpu.VMEM((owners * 16, 2 * lanes), bf16)],
        compiler_params=pltpu.CompilerParams(vmem_limit_bytes=40 * 1024 * 1024),
        cost_estimate=pl.CostEstimate(flops=4 * 10**9, bytes_accessed=2_000_000, transcendentals=0),
    )(held, held)


def attend_kernel(sub, q_ref, own_ref, peer_ref, new_ref, bias_ref, out_ref, value_ref, key_ref, score_ref):
    latent = 4 * lanes
    rows = own_ref.shape[0] // 4
    pages = 24
    half = rows * pages
    prefix = 2 * half

    @pl.when(pl.program_id(0) == 0)
    def build():
        src = iota((64, lanes), 1)
        dst = iota((64, lanes), 0)
        group = iota((8, lanes), 1) // 16 == iota((8, lanes), 0)
        for side, ref in enumerate((own_ref, peer_ref)):
            at = side * half
            rope_keys = jnp.zeros((64, half), f32)
            for quarter in range(4):
                block = ref[quarter * rows : (quarter + 1) * rows].astype(f32)
                part = block[:, :pages].reshape(half, lanes)
                value_ref[at : at + half, quarter * lanes : (quarter + 1) * lanes] = part.astype(bf16)
                key_ref[quarter * lanes : (quarter + 1) * lanes, at : at + half] = part.T.astype(bf16)
                pieces = [
                    jnp.where(group[None], block[:, 25 + k : 26 + k], 0.0) for k in range(3)
                ]
                rope = jnp.concatenate(pieces, axis=1).reshape(half, lanes).astype(bf16)
                place = picks((dst // 16 == quarter) & (dst % 16 == src % 16))
                rope_keys += mm_last(place, rope)
            key_ref[latent : latent + 64, at : at + half] = rope_keys.astype(bf16)
        fresh = new_ref[...].astype(f32)
        blank = jnp.zeros((64, latent), f32)
        part = jnp.concatenate([fresh[:, :latent], blank], axis=0)
        value_ref[prefix:, :] = part.astype(bf16)
        key_ref[:latent, prefix:] = part.T.astype(bf16)
        rope = jnp.concatenate([fresh[:, latent:], jnp.zeros((64, 64), f32)], axis=0)
        key_ref[latent : latent + 64, prefix:] = rope.T.astype(bf16)
        key_ref[latent + 64 :, :] = bias_ref[...]

    count = q_ref.shape[0] // sub
    factor = jnp.float32(score_scale * log2_e)
    for part in range(count):
        at = slice(part * sub, (part + 1) * sub)
        scores = mm(q_ref[at, :], key_ref[...])
        top = jnp.max(scores, axis=1, keepdims=True)
        weight = jnp.exp2((scores - top) * factor)
        total = jnp.sum(weight, axis=1, keepdims=True)
        summed = mm(weight.astype(bf16), value_ref[...])
        out_ref[at, :] = (summed * (1.0 / total)).astype(bf16)


def attend(queries, own, peer, fresh, bias, block=512, sub=256):
    count, width = queries.shape
    keys = bias.shape[1]
    latent = 4 * lanes
    whole = lambda a: pl.BlockSpec(a.shape, lambda i: (0,) * a.ndim)
    return pl.pallas_call(
        functools.partial(attend_kernel, sub),
        grid=(count // block,),
        in_specs=[
            pl.BlockSpec((block, width), lambda i: (i, 0)),
            whole(own),
            whole(peer),
            whole(fresh),
            whole(bias),
        ],
        out_specs=pl.BlockSpec((block, latent), lambda i: (i, 0)),
        out_shape=jax.ShapeDtypeStruct((count, latent), bf16),
        scratch_shapes=[
            pltpu.VMEM((keys, latent), bf16),
            pltpu.VMEM((width, keys), bf16),
            pltpu.VMEM((8, lanes), f32),
        ],
        compiler_params=pltpu.CompilerParams(vmem_limit_bytes=56 * 1024 * 1024),
        cost_estimate=pl.CostEstimate(
            flops=2 * count * keys * (width + latent), bytes_accessed=11_000_000, transcendentals=count * keys
        ),
    )(queries, own, peer, fresh, bias)


def body(
    q_latent,
    q_rope,
    new_latent,
    pool_pages,
    page_owner,
    page_slot,
    prefix_len,
    partner,
    dest_slot,
    decode_cache,
):
    stretch, heads, latent = q_latent.shape
    rope = q_rope.shape[1] // heads
    slots, page, width = pool_pages.shape
    most = page_owner.shape[1]
    rows = page // 2
    core = lax.axis_index("pd")

    gap = jnp.zeros((1, 8), jnp.int32)
    meta = jnp.concatenate(
        [page_owner, gap, page_slot, gap, partner[:, None], jnp.zeros((1, lanes - 65), jnp.int32)], axis=1
    ).astype(bf16)
    outgoing = spread(core.astype(jnp.int32)[None], pool_pages, new_latent, meta)
    held = lax.all_to_all(outgoing, "pool", split_axis=0, concat_axis=0, tiled=True)

    token = jnp.arange(stretch, dtype=jnp.int32)
    mark = jnp.broadcast_to(
        (token[:, None] == token[None, :]).astype(bf16)[:, None, :], (stretch, heads, stretch)
    )
    queries = jnp.concatenate([q_latent, q_rope.reshape(stretch, heads, rope), mark], axis=2)
    queries = queries.reshape(stretch * heads, latent + rope + stretch)
    key = jnp.arange(rows * most, dtype=jnp.int32)
    spot = (key % most) * page + key // most
    spots = jnp.concatenate([spot + rows * core, spot + rows * (1 - core)])
    seen = jnp.broadcast_to((spots < prefix_len[0])[None, :], (stretch, 2 * rows * most))
    late = jnp.arange(2 * stretch, dtype=jnp.int32)
    causal = late[None, :] <= token[:, None]
    bias = jnp.where(jnp.concatenate([seen, causal], axis=1), 0.0, hidden).astype(bf16)

    replies = collect(held)
    own = lax.all_to_all(replies, "pool", split_axis=0, concat_axis=0, tiled=True)
    peer = lax.ppermute(own, "pd", [(0, 1), (1, 0)])
    context = attend(queries, own, peer, new_latent, bias).reshape(stretch, heads, latent)

    tails = jnp.where(core == 0, jnp.stack([own[:, 24:], peer[:, 24:]]), jnp.stack([peer[:, 24:], own[:, 24:]]))
    tails = tails.reshape(2, 4, rows, 8, lanes)
    first = tails[:, :, :, 0].transpose(0, 2, 1, 3).reshape(page, latent)
    second = tails[:, :, :, 4, :16].transpose(0, 2, 1, 3).reshape(page, rope)
    arrived = jnp.concatenate([first, second], axis=1)
    decode_out = lax.dynamic_update_slice(decode_cache, arrived[None], (dest_slot[0], 0, 0))
    return (context, decode_out)


def solution(mesh):
    placed = (
        P("pool", "pd", None),
        P("pool", "pd"),
        P("pool", None),
        P("pool", None, None),
        P("pool", None),
        P("pool", None),
        P("pool"),
        P("pool"),
        P("pool"),
        P("pool", None, None),
    )
    return jax.shard_map(
        body,
        mesh=mesh,
        in_specs=placed,
        out_specs=(P("pool", "pd", None), P("pool", None, None)),
        check_vma=False,
    )
```

time: 595 us -> 135 us (0.23)
  waiting for transfers between devices: 414 us -> 25.5 us
  matrix products: 56.1 us -> 0 us
  other arithmetic: 57.2 us -> 8.71 us
  Pallas kernels: 0 us -> 40.8 us
  blocking collectives: 0 us -> 37.8 us
  starting transfers between devices: 38.8 us -> 13.8 us
  local copies, waits for them, and re-layouts: 20.7 us -> 5.03 us
    all_to_all x3 -> x1, waiting for transfers between devices: 414 us -> 25.5 us  [body(): lax.all_to_all(replies, 'pool', split_axis=0, concat_axis=0, tiled=True)]
    dot_general x8 -> x0, matrix products: 56.1 us -> none  [the longest x4 30.2 us: absorb(): jnp.einsum('qd,kd->qk', queries, keys, preferred_element_type=jnp.float32)]
    pallas_call x0 -> x3, Pallas kernels: none -> 40.8 us  [the longest x1 29.6 us: attend(): pl.pallas_call(functools.partial(attend_kernel, sub), grid=(count // bloc...]
    all_to_all x0 -> x1, blocking collectives: none -> 37.8 us  [body(): lax.all_to_all(outgoing, 'pool', split_axis=0, concat_axis=0, tiled=True)]
    all_to_all x3 -> x1, starting transfers between devices: 38.8 us -> 8.98 us  [body(): lax.all_to_all(replies, 'pool', split_axis=0, concat_axis=0, tiled=True)]
    reduce_sum x6 -> x0, other arithmetic: 22.7 us -> none  [the longest x4 16.3 us: absorb(): total = total * shrink + jnp.sum(weight, axis=1)]
    select_n x7 -> x1, other arithmetic: 21.6 us -> 0.05 us  [body(): jnp.where(core == 0, jnp.stack([own[:, 24:], peer[:, 24:]]), jnp.stack([p...]
    gather x2 -> x0, local copies, waits for them, and re-layouts: 13.5 us -> none  [the longest x1 7.43 us: body(): picked = jnp.take(pool_pages, jnp.clip(asked, 0, slots - 1), axis=0)]
  transfers between devices with their start and end apart: 3 -> 2, of which waited for: 3 -> 1; matrix products, arithmetic and copies ran while one was open for 8% -> 6% of each run, Pallas kernels for 0% -> 0%
where the time goes in v1:
time: 135 us; the launch traced here: 134 us
  Pallas kernels  40.8 us (30%)
  blocking collectives  37.8 us (28%)
  waiting for transfers between devices  25.5 us (19%)
  starting transfers between devices  13.8 us (10%)
  other arithmetic  8.71 us (6%)
  local copies, waits for them, and re-layouts  5.03 us (4%)
  between operations  2.81 us (2%)
    all_to_all x1, blocking collectives, body(): lax.all_to_all(outgoing, 'pool', split_axis=0, concat_axis=0, tiled=True)  37.8 us
    pallas_call x1, Pallas kernels, attend(): pl.pallas_call(functools.partial(attend_kernel, sub), grid=(count // bloc...  29.6 us
    all_to_all x1, waiting for transfers between devices, body(): lax.all_to_all(replies, 'pool', split_axis=0, concat_axis=0, tiled=True)  25.5 us
    pallas_call x1, Pallas kernels, collect(): pl.pallas_call(functools.partial(collect_kernel, block), grid=(owners //...  9.49 us
    all_to_all x1, starting transfers between devices, body(): lax.all_to_all(replies, 'pool', split_axis=0, concat_axis=0, tiled=True)  8.98 us
    concatenate x1, other arithmetic, body(): jnp.concatenate([q_latent, q_rope.reshape(stretch, heads, rope), mark], a...  6.55 us
    ppermute x1, starting transfers between devices, body(): peer = lax.ppermute(own, 'pd', [(0, 1), (1, 0)])  4.8 us
  transfers between devices with their start and end apart: 2, of which 1 were waited for; matrix products, arithmetic and copies ran while one was open for 6% of the time, Pallas kernels for 0%

profile of v1, /device:TPU:1, one launch (start us, length us, event | category | flops | bytes accessed | tf_op | source)
XLA Modules:
  0.0 134.4 jit_solution(17519249086981655137)
XLA Ops:
  0.6 0.7 convert.16
  1.3 0.7 convert.17
  2.6 0.1 concatenate.47.meta_ref
  2.7 0.0 copy-start
  2.7 1.3 copy-done
  4.1 0.0 copy-start.1
  4.1 0.9 copy-done.1
  4.9 1.7 %shard_map.113 = bf16[128,24,128]{2,1,0:T(8,128)(2,1)S(1)} custom-call(s32[1]{0:T(128)} %bitcast.2.half_ref, bf16[16,64,576]{2,1,0:T(8,128)(2,1)S(1)} %copy-done, bf16[64,576]{1,0:T(8,128)(2,1)S(1)} %copy-done.1, bf16[1,128]{1,0:T(2,128)(2,1)S(1)} %concatenate.47.meta_ref), custom_call_target="tpu_custom_call" | custom-call | flops 1000000000 | bytes 1500000 | tf_op jit(solution)/shard_map/pallas_call | solution.py:77
  6.7 37.8 %all_to_all.10.all_ref.mine_ref = bf16[128,24,128]{2,1,0:T(8,128)(2,1)S(1)} all-to-all(bf16[128,24,128]{2,1,0:T(8,128)(2,1)S(1)} %shard_map.113), channel_id=1, replica_groups=mesh['pool'=128,'pd'=2] {'pool'}, dimensions={0} | all-to-all | bytes 1572864 | tf_op jit(solution)/shard_map/all_to_all | solution.py:267
  44.5 0.0 copy-start.5
  44.5 9.5 %shard_map.114 = bf16[128,32,128]{2,1,0:T(8,128)(2,1)} custom-call(bf16[128,24,128]{2,1,0:T(8,128)(2,1)S(1)} %all_to_all.10.all_ref.mine_ref, bf16[128,24,128]{2,1,0:T(8,128)(2,1)S(1)} %all_to_all.10.all_ref.mine_ref), custom_call_target="tpu_custom_call" | custom-call | flops 4000000000 | bytes 2000000 | tf_op jit(solution)/shard_map/pallas_call | solution.py:151
  54.0 9.0 %all-to-all-start.1 = ((bf16[128,32,128]{2,1,0:T(8,128)(2,1)}), bf16[128,32,128]{2,1,0:T(8,128)(2,1)S(1)}, u32[]{:S(2)}, u32[]{:S(2)}) async-start(bf16[128,32,128]{2,1,0:T(8,128)(2,1)} %shard_map.114), calls=%async_computation.1 | async-start | bytes 2097152 | tf_op jit(solution)/shard_map/all_to_all | solution.py:284
  63.7 25.5 %all-to-all-done.1.own_ref = bf16[128,32,128]{2,1,0:T(8,128)(2,1)S(1)} async-done(((bf16[128,32,128]{2,1,0:T(8,128)(2,1)}), bf16[128,32,128]{2,1,0:T(8,128)(2,1)S(1)}, u32[]{:S(2)}, u32[]{:S(2)}) %all-to-all-start.1) | async-done | bytes 1048608 | tf_op jit(solution)/shard_map/all_to_all | solution.py:284
  89.2 0.0 copy-start.2
  89.2 4.8 %collective-permute-start = (bf16[128,32,128]{2,1,0:T(8,128)(2,1)S(1)}, bf16[128,32,128]{2,1,0:T(8,128)(2,1)}, u32[]{:S(2)}, u32[]{:S(2)}) collective-permute-start(bf16[128,32,128]{2,1,0:T(8,128)(2,1)S(1)} %all-to-all-done.1.own_ref), channel_id=1, source_target_pairs={{0,1},{1,0},{2,3},{3,2},{4,5},{5,4},{6,7},{7,6},{8,9},{9,8},{10,11... | collective-permute-start | bytes 3145736 | tf_op jit(solution)/shard_map/ppermute | solution.py:285
  94.0 0.0 copy-done.5
  94.0 1.1 concatenate.42
  95.8 0.7 select_convert_fusion.bias_ref
  96.5 0.1 broadcast_in_dim.16
  96.7 0.0 copy-start.4
  96.7 6.6 %pad_maximum_fusion.q_ref = bf16[4096,640]{1,0:T(8,128)(2,1)} fusion(bf16[4096,64]{1,0:T(8,128)(2,1)S(1)} %bitcast.33, bf16[4096,64]{1,0:T(8,128)(2,1)S(1)} %concatenate.42, bf16[4096,512]{1,0:T(8,128)(2,1)} %bitcast.32), kind=kLoop, calls=%fused_computation | loop fusion | flops 15728640 | bytes 10485760 | tf_op jit(solution)/shard_map/concatenate | solution.py:273
  103.2 0.0 copy-done.2
  103.3 0.0 collective-permute-done.peer_ref
  103.3 1.0 slice.19
  104.4 0.1 maximum_select_fusion
  104.4 0.1 copy.27
  104.5 0.1 reshape.124
  104.6 0.1 copy.28
  104.8 0.0 copy-done.4
  104.8 0.0 copy-start.3
  104.9 29.6 %shard_map.115 = bf16[4096,512]{1,0:T(8,128)(2,1)} custom-call(bf16[4096,640]{1,0:T(8,128)(2,1)} %pad_maximum_fusion.q_ref, bf16[128,32,128]{2,1,0:T(8,128)(2,1)} %copy-done.2, bf16[128,32,128]{2,1,0:T(8,128)(2,1)} %collective-permute-done.peer_ref, bf16[64,576]{1,0:T(8,128)(2,1)} %new_ref.3, bf16[64,1664]{1,0:T(8,128)(2,1)} %select_convert_fusion.bias_ref), custom_call_target="tpu_custom_call" | custom-call | flops 15703474176 | bytes 11000000 | tf_op jit(solution)/shard_map/pallas_call | solution.py:219
  134.4 0.0 copy-done.3
  (16 shorter events, 0.3 us)
Async XLA Ops:
  2.7 1.3 copy-start
  4.1 0.9 copy-start.1
  44.5 49.5 %copy-start.5 = (bf16[64,4096]{1,0:T(8,128)(2,1)S(1)}, bf16[64,4096]{1,0:T(8,128)(2,1)}, u32[]{:S(2)}) copy-start(bf16[64,4096]{1,0:T(8,128)(2,1)} %param.11) | copy-start | bytes 1572868
  54.0 35.2 %all-to-all-start.1 = ((bf16[128,32,128]{2,1,0:T(8,128)(2,1)}), bf16[128,32,128]{2,1,0:T(8,128)(2,1)S(1)}, u32[]{:S(2)}, u32[]{:S(2)}) async-start(bf16[128,32,128]{2,1,0:T(8,128)(2,1)} %shard_map.114), calls=%async_computation.1 | async-start | bytes 2097152 | tf_op jit(solution)/shard_map/all_to_all | solution.py:284
  89.2 14.1 %copy-start.2 = (bf16[128,32,128]{2,1,0:T(8,128)(2,1)}, bf16[128,32,128]{2,1,0:T(8,128)(2,1)S(1)}, u32[]{:S(2)}) copy-start(bf16[128,32,128]{2,1,0:T(8,128)(2,1)S(1)} %all-to-all-done.1.own_ref) | copy-start | bytes 3145732
  89.2 14.1 %collective-permute-start = (bf16[128,32,128]{2,1,0:T(8,128)(2,1)S(1)}, bf16[128,32,128]{2,1,0:T(8,128)(2,1)}, u32[]{:S(2)}, u32[]{:S(2)}) collective-permute-start(bf16[128,32,128]{2,1,0:T(8,128)(2,1)S(1)} %all-to-all-done.1.own_ref), channel_id=1, source_target_pairs={{0,1},{1,0},{2,3},{3,2},{4,5},{5,4},{6,7},{7,6},{8,9},{9,8},{10,11... | collective-permute-start | bytes 3145736 | tf_op jit(solution)/shard_map/ppermute | solution.py:285
  96.7 8.1 %copy-start.4 = (bf16[8,64,576]{2,1,0:T(8,128)(2,1)S(1)}, bf16[8,64,576]{2,1,0:T(8,128)(2,1)}, u32[]{:S(2)}) copy-start(bf16[8,64,576]{2,1,0:T(8,128)(2,1)} %param.19) | copy-start | bytes 1769476
  104.8 29.6 %copy-start.3 = (bf16[8,64,576]{2,1,0:T(8,128)(2,1)}, bf16[8,64,576]{2,1,0:T(8,128)(2,1)S(1)}, u32[]{:S(2)}) copy-start(bf16[8,64,576]{2,1,0:T(8,128)(2,1)S(1)} %fusion) | copy-start | bytes 1769476

commit v2 on v0

v2 whole, which is shorter than its diff:
```python
import functools

import jax
import jax.numpy as jnp
from jax import lax
from jax.experimental import pallas as pl
from jax.experimental.pallas import tpu as pltpu
from jax.sharding import PartitionSpec as P

score_scale = 192.0 ** (-0.5)
log2_e = 1.4426950408889634
hidden = -1e30
lanes = 128
f32 = jnp.float32
bf16 = jnp.bfloat16


def iota(shape, axis):
    return lax.broadcasted_iota(jnp.int32, shape, axis)


def picks(condition):
    return jnp.where(condition, jnp.float32(1.0), jnp.float32(0.0)).astype(bf16)


def mm(a, b):
    return lax.dot_general(a, b, (((1,), (0,)), ((), ())), preferred_element_type=f32)


def mm_first(a, b):
    return lax.dot_general(a, b, (((0,), (0,)), ((), ())), preferred_element_type=f32)


def mm_last(a, b):
    return lax.dot_general(a, b, (((1,), (1,)), ((), ())), preferred_element_type=f32)


def spread_kernel(partner_ref, pages_ref, new_ref, owner_ref, slot_ref, out_ref):
    slots = pages_ref.shape[0]
    rows = out_ref.shape[1]
    begin = pl.multiple_of(lax.axis_index("pd") * (2 * rows) + pl.program_id(0) * rows, rows)
    held = 24
    pages = pages_ref[:, pl.ds(begin, rows), :].reshape(slots * rows, pages_ref.shape[2])
    fresh = new_ref[pl.ds(begin, rows), :]
    latent = 4 * lanes
    total = rows * held
    out_row = iota((total, 1), 0)
    out_r = out_row // held
    out_k = out_row % held
    in_row = iota((total, slots * rows), 1)
    in_r = in_row % rows
    in_s = in_row // rows
    same = in_r == out_r
    take_latent = picks(same & (in_s == out_k))
    take_rope = picks(same & (in_s // 8 == out_k - 17))
    new_same = iota((total, rows), 1) == out_r
    take_new = picks(new_same & (out_k == 16))
    take_new_rope = picks(new_same & (out_k == 19))
    src = iota((64, latent), 0)
    dst = iota((64, latent), 1)
    tile = picks((src // 16 == dst // lanes) & (src % 16 == dst % 16))
    group = (iota((slots * rows, latent), 1) % lanes) // 16
    slot = iota((slots * rows, latent), 0) // rows
    rope = mm(pages[:, latent:], tile)
    rope = jnp.where(group == slot % 8, rope, 0.0).astype(bf16)
    new_rope = mm(fresh[:, latent:], tile).astype(bf16)
    result = mm(take_latent, pages[:, :latent]) + mm(take_rope, rope)
    result += mm(take_new, fresh[:, :latent]) + mm(take_new_rope, new_rope)
    asked = owner_ref.shape[1]
    lane = iota((asked, lanes), 1)
    at = iota((asked, lanes), 0)
    meta = mm(owner_ref[...].astype(f32).astype(bf16), picks(lane == at))
    meta += mm(slot_ref[...].astype(f32).astype(bf16), picks(lane == at + 32))
    meta = jnp.where(iota((1, lanes), 1) == 64, partner_ref[0].astype(f32), meta)
    for quarter in range(4):
        part = result[:, quarter * lanes : (quarter + 1) * lanes]
        part = jnp.where(out_k == 20, meta, part)
        out_ref[quarter] = part.reshape(rows, held, lanes).astype(bf16)


def spread(partner, pages, fresh, owner, slot):
    slots, page, width = pages.shape
    rows = page // 4
    whole = lambda a: pl.BlockSpec(a.shape, lambda i: (0,) * a.ndim)
    out = pl.pallas_call(
        spread_kernel,
        grid=(2,),
        in_specs=[
            pl.BlockSpec(memory_space=pltpu.SMEM),
            whole(pages),
            whole(fresh),
            whole(owner),
            whole(slot),
        ],
        out_specs=pl.BlockSpec((4, rows, 24, lanes), lambda i: (0, i, 0, 0)),
        out_shape=jax.ShapeDtypeStruct((4, 2 * rows, 24, lanes), bf16),
        compiler_params=pltpu.CompilerParams(vmem_limit_bytes=60 * 1024 * 1024),
        cost_estimate=pl.CostEstimate(flops=10**9, bytes_accessed=1_500_000, transcendentals=0),
    )(partner, pages, fresh, owner, slot)
    return out.reshape(8 * rows, 24, lanes)


def collect_kernel(pages, group, all_ref, out_ref, rows_ref, table_ref, stage_ref):
    owners, held, _ = all_ref.shape
    slots = 16
    size = 32
    rows_ref[...] = all_ref[...].astype(f32).reshape(owners * held, lanes)
    src = iota((lanes, lanes), 0)
    dst = iota((lanes, lanes), 1)
    tile = picks(src % 16 == dst % 16)
    lane = iota((owners, lanes), 1)
    for slot in range(slots):
        at = slice(slot * owners, (slot + 1) * owners)
        table_ref[at, :lanes] = rows_ref[pl.ds(slot, owners, stride=held), :].astype(bf16)
        piece = rows_ref[pl.ds(17 + slot // 8, owners, stride=held), :]
        piece = jnp.where(lane // 16 == slot % 8, piece, 0.0).astype(bf16)
        table_ref[at, lanes:] = mm(piece, tile).astype(bf16)
    meta = rows_ref[pl.ds(20, owners, stride=held), :]
    blank = jnp.zeros((owners, lanes), f32)
    ropes = [blank] * (pages // 8)
    for start in range(0, pages, group):
        wanted = []
        for place in range(start, start + group):
            owner = picks(meta[:, place : place + 1] == lane.astype(f32))
            slot = jnp.broadcast_to(meta[:, 32 + place : 33 + place], (owners, lanes)).astype(bf16)
            wanted.append(
                jnp.concatenate(
                    [jnp.where(slot == jnp.bfloat16(k), owner, jnp.bfloat16(0)) for k in range(slots)], axis=1
                )
            )
        found = mm(jnp.concatenate(wanted, axis=0), table_ref[...])
        for k in range(group):
            place = start + k
            got = found[k * owners : (k + 1) * owners]
            stage_ref[pl.ds(place, owners, stride=size), :] = got[:, :lanes]
            ropes[place // 8] += jnp.where(lane // 16 == place % 8, got[:, lanes:], 0.0)
    comes = picks(meta[:, 64:65].astype(jnp.int32) == lane)
    arriving = mm_first(comes, rows_ref[pl.ds(16, owners, stride=held), :].astype(bf16))
    arriving_rope = mm_first(comes, rows_ref[pl.ds(19, owners, stride=held), :].astype(bf16))
    tail = [arriving] + ropes + [arriving_rope]
    tail += [blank] * (size - pages - len(tail))
    for k, piece in enumerate(tail):
        stage_ref[pl.ds(pages + k, owners, stride=size), :] = piece
    out_ref[...] = stage_ref[...].reshape(owners, size, lanes).astype(bf16)


def collect(held, pages):
    owners = held.shape[0]
    return pl.pallas_call(
        functools.partial(collect_kernel, pages, 4),
        in_specs=[pl.BlockSpec(memory_space=pltpu.VMEM)],
        out_specs=pl.BlockSpec(memory_space=pltpu.VMEM),
        out_shape=jax.ShapeDtypeStruct((owners, 32, lanes), bf16),
        scratch_shapes=[
            pltpu.VMEM((owners * held.shape[1], lanes), f32),
            pltpu.VMEM((owners * 16, 2 * lanes), bf16),
            pltpu.VMEM((owners * 32, lanes), f32),
        ],
        compiler_params=pltpu.CompilerParams(vmem_limit_bytes=40 * 1024 * 1024),
        cost_estimate=pl.CostEstimate(flops=4 * 10**9, bytes_accessed=1_500_000, transcendentals=0),
    )(held)


factor = score_scale * log2_e


def fresh_kernel(sub, q_ref, new_ref, acc_ref, stat_ref, value_ref, key_ref):
    latent = 4 * lanes

    @pl.when(pl.program_id(0) == 0)
    def build():
        fresh = new_ref[...].astype(f32)
        part = jnp.concatenate([fresh[:, :latent], jnp.zeros((64, latent), f32)], axis=0)
        value_ref[...] = part.astype(bf16)
        key_ref[:latent, :] = part.T.astype(bf16)
        rope = jnp.concatenate([fresh[:, latent:], jnp.zeros((64, 64), f32)], axis=0)
        key_ref[latent : latent + 64, :] = rope.T.astype(bf16)
        token = iota((64, lanes), 0)
        late = iota((64, lanes), 1)
        key_ref[latent + 64 :, :] = jnp.where(late <= token, 0.0, hidden).astype(bf16)

    for part in range(q_ref.shape[0] // sub):
        at = slice(part * sub, (part + 1) * sub)
        scores = mm(q_ref[at, :], key_ref[...])
        top = jnp.max(scores, axis=1, keepdims=True)
        weight = jnp.exp2((scores - top) * jnp.float32(factor))
        total = jnp.sum(weight, axis=1, keepdims=True)
        acc_ref[at, :] = mm(weight.astype(bf16), value_ref[...])
        stat_ref[at, :] = jnp.where(iota((sub, lanes), 1) < 64, top, total)


def attend_fresh(queries, fresh, block=512, sub=256):
    count, width = queries.shape
    latent = 4 * lanes
    return pl.pallas_call(
        functools.partial(fresh_kernel, sub),
        grid=(count // block,),
        in_specs=[
            pl.BlockSpec((block, width), lambda i: (i, 0)),
            pl.BlockSpec(fresh.shape, lambda i: (0, 0)),
        ],
        out_specs=[
            pl.BlockSpec((block, latent), lambda i: (i, 0)),
            pl.BlockSpec((block, lanes), lambda i: (i, 0)),
        ],
        out_shape=[
            jax.ShapeDtypeStruct((count, latent), f32),
            jax.ShapeDtypeStruct((count, lanes), f32),
        ],
        scratch_shapes=[pltpu.VMEM((lanes, latent), bf16), pltpu.VMEM((width, lanes), bf16)],
        compiler_params=pltpu.CompilerParams(vmem_limit_bytes=40 * 1024 * 1024),
        cost_estimate=pl.CostEstimate(flops=5 * 10**9, bytes_accessed=16_000_000, transcendentals=count * lanes),
    )(queries, fresh)


def attend_kernel(
    pages,
    sub,
    chunk,
    length_ref,
    dest_ref,
    q_ref,
    own_ref,
    peer_ref,
    acc_ref,
    stat_ref,
    cache_ref,
    out_ref,
    decode_ref,
    key_ref,
    score_ref,
    arrive_ref,
):
    latent = 4 * lanes
    rows = own_ref.shape[0] // 4
    half = rows * pages
    keys = 2 * half
    step = pl.program_id(0)

    @pl.when(step == 0)
    def build():
        core = lax.axis_index("pd")
        src = iota((lanes, lanes), 0)
        dst = iota((lanes, lanes), 1)
        group = iota((8, lanes), 1) // 16 == iota((8, lanes), 0)
        key = iota((half, 1), 0)
        row = key // pages
        place = (key - row * pages) * 64 + row
        for side, ref in enumerate((own_ref, peer_ref)):
            at = slice(side * half, (side + 1) * half)
            spot = pl.multiple_of((core if side == 0 else 1 - core) * rows, rows)
            rope_keys = jnp.zeros((half, lanes), f32)
            arrived_rope = jnp.zeros((rows, lanes), f32)
            for quarter in range(4):
                cols = slice(quarter * lanes, (quarter + 1) * lanes)
                block = ref[quarter * rows : (quarter + 1) * rows].astype(f32)
                key_ref[at, cols] = block[:, :pages].reshape(half, lanes).astype(bf16)
                tail = block[:, pages:]
                pieces = [jnp.where(group[None], tail[:, 1 + k : 2 + k], 0.0) for k in range(pages // 8)]
                rope = jnp.concatenate(pieces, axis=1).reshape(half, lanes).astype(bf16)
                put = picks((dst // 16 == quarter) & (dst % 16 == src % 16))
                rope_keys += mm(rope, put)
                arrive_ref[pl.ds(spot, rows), cols] = tail[:, 0, :]
                last = jnp.where(iota((rows, lanes), 1) < 16, tail[:, 1 + pages // 8, :], 0.0)
                arrived_rope += mm(last.astype(bf16), put)
            arrive_ref[pl.ds(spot, rows), latent:] = arrived_rope[:, :64]
            bias = jnp.where(place + spot < length_ref[0], 0.0, hidden)
            joined = jnp.where(iota((half, lanes), 1) < 64, rope_keys, bias)
            key_ref[at, latent:] = joined.astype(bf16)

    count = q_ref.shape[0] // sub
    scale = jnp.float32(factor)

    def score(part):
        at = slice(part * sub, (part + 1) * sub)
        top = None
        for begin in range(0, keys, chunk):
            found = mm_last(q_ref[at, :], key_ref[begin : begin + chunk, :])
            score_ref[part % 2, :, begin : begin + chunk] = found
            for k in range(0, chunk, lanes):
                piece = found[:, k : k + lanes]
                top = piece if top is None else jnp.maximum(top, piece)
        return jnp.maximum(jnp.max(top, axis=1, keepdims=True), stat_ref[at, :1])

    def finish(part, top):
        at = slice(part * sub, (part + 1) * sub)
        summed = None
        total = None
        for begin in range(0, keys, chunk):
            weight = jnp.exp2((score_ref[part % 2, :, begin : begin + chunk] - top) * scale)
            for k in range(0, chunk, lanes):
                piece = weight[:, k : k + lanes]
                total = piece if total is None else total + piece
            product = mm(weight.astype(bf16), key_ref[begin : begin + chunk, :latent])
            summed = product if summed is None else summed + product
        shrink = jnp.exp2((stat_ref[at, :1] - top) * scale)
        total = jnp.sum(total, axis=1, keepdims=True) + shrink * stat_ref[at, 64:65]
        summed = summed + shrink * acc_ref[at, :]
        out_ref[at, :] = (summed * (1.0 / total)).astype(bf16)

    top = score(0)
    for part in range(count):
        after = score(part + 1) if part + 1 < count else None
        finish(part, top)
        top = after

    share = cache_ref.shape[0]
    for k in range(share):
        hit = dest_ref[0] == step * share + k
        decode_ref[k] = jnp.where(hit, arrive_ref[...], cache_ref[k].astype(f32)).astype(bf16)


def attend(length, dest, queries, own, peer, acc, stat, cache, pages, block=1024, sub=256, chunk=256):
    count, width = queries.shape
    latent = 4 * lanes
    keys = 64 * pages
    steps = count // block
    whole = lambda a: pl.BlockSpec(a.shape, lambda i: (0,) * a.ndim)
    strip = lambda w: pl.BlockSpec((block, w), lambda i: (i, 0))
    scalar = pl.BlockSpec(memory_space=pltpu.SMEM)
    share = pl.BlockSpec((cache.shape[0] // steps,) + cache.shape[1:], lambda i: (i, 0, 0))
    return pl.pallas_call(
        functools.partial(attend_kernel, pages, sub, chunk),
        grid=(steps,),
        in_specs=[scalar, scalar, strip(width), whole(own), whole(peer), strip(latent), strip(lanes), share],
        out_specs=[strip(latent), share],
        out_shape=[
            jax.ShapeDtypeStruct((count, latent), bf16),
            jax.ShapeDtypeStruct(cache.shape, bf16),
        ],
        scratch_shapes=[
            pltpu.VMEM((keys, width), bf16),
            pltpu.VMEM((2, sub, keys), f32),
            pltpu.VMEM(cache.shape[1:], f32),
        ],
        compiler_params=pltpu.CompilerParams(vmem_limit_bytes=48 * 1024 * 1024),
        cost_estimate=pl.CostEstimate(
            flops=2 * count * keys * (width + latent), bytes_accessed=20_000_000, transcendentals=count * keys
        ),
    )(length, dest, queries, own, peer, acc, stat, cache)


def body(
    q_latent,
    q_rope,
    new_latent,
    pool_pages,
    page_owner,
    page_slot,
    prefix_len,
    partner,
    dest_slot,
    decode_cache,
):
    stretch, heads, latent = q_latent.shape
    rope = q_rope.shape[1] // heads

    outgoing = spread(partner, pool_pages, new_latent, page_owner, page_slot)
    held = lax.all_to_all(outgoing, "pool", split_axis=0, concat_axis=0, tiled=True)

    token = jnp.arange(stretch, dtype=jnp.int32)
    mark = jnp.broadcast_to(
        (token[:, None] == token[None, :]).astype(bf16)[:, None, :], (stretch, heads, stretch)
    )
    queries = jnp.concatenate([q_latent, q_rope.reshape(stretch, heads, rope), mark], axis=2)
    queries = queries.reshape(stretch * heads, latent + rope + stretch)
    acc, stat = attend_fresh(queries, new_latent)
    held, acc, stat = lax.optimization_barrier((held, acc, stat))

    pages = page_owner.shape[1]
    own = lax.all_to_all(collect(held, pages), "pool", split_axis=0, concat_axis=0, tiled=True)
    peer = lax.ppermute(own, "pd", [(0, 1), (1, 0)])
    context, decode_out = attend(prefix_len, dest_slot, queries, own, peer, acc, stat, decode_cache, pages)
    return (context.reshape(stretch, heads, latent), decode_out)


def solution(mesh):
    placed = (
        P("pool", "pd", None),
        P("pool", "pd"),
        P("pool", None),
        P("pool", None, None),
        P("pool", None),
        P("pool", None),
        P("pool"),
        P("pool"),
        P("pool"),
        P("pool", None, None),
    )
    return jax.shard_map(
        body,
        mesh=mesh,
        in_specs=placed,
        out_specs=(P("pool", "pd", None), P("pool", None, None)),
        check_vma=False,
    )
```

time: 595 us -> 114 us (0.19)
  waiting for transfers between devices: 414 us -> 6.17 us
  matrix products: 56.1 us -> 0 us
  other arithmetic: 57.2 us -> 4.29 us
  Pallas kernels: 0 us -> 40.8 us
  blocking collectives: 0 us -> 35 us
  starting transfers between devices: 38.8 us -> 21.1 us
  local copies, waits for them, and re-layouts: 20.7 us -> 3.65 us
    all_to_all x2 -> x0, waiting for transfers between devices: 212 us -> none  [the longest x1 208 us: body(): lax.all_to_all(picked, 'pool', split_axis=0, concat_axis=0, tiled=True)]
    all_to_all x1, waiting for transfers between devices: 202 us -> 5.18 us  [body(): lax.all_to_all(outgoing, 'pool', split_axis=0, concat_axis=0, tiled=True)]
    dot_general x8 -> x0, matrix products: 56.1 us -> none  [the longest x4 30.2 us: absorb(): jnp.einsum('qd,kd->qk', queries, keys, preferred_element_type=jnp.float32)]
    pallas_call x0 -> x4, Pallas kernels: none -> 40.8 us  [the longest x1 23.1 us: attend(): pl.pallas_call(functools.partial(attend_kernel, pages, sub, chunk), grid=...]
    all_to_all x0 -> x1, blocking collectives: none -> 35 us  [body(): lax.all_to_all(collect(held, pages), 'pool', split_axis=0, concat_axis=0,...]
    all_to_all x2 -> x0, starting transfers between devices: 29 us -> none  [the longest x1 16.3 us: body(): lax.all_to_all(requests, 'pool', split_axis=0, concat_axis=0, tiled=True)]
    reduce_sum x6 -> x0, other arithmetic: 22.7 us -> none  [the longest x4 16.3 us: absorb(): total = total * shrink + jnp.sum(weight, axis=1)]
    select_n x7 -> x0, other arithmetic: 21.6 us -> none  [the longest x1 10.6 us: body(): jnp.where(usable[:, :, None, None], picked, jnp.zeros((), pool_pages.dtype))]
  transfers between devices with their start and end apart: 3 -> 2, of which waited for: 3 -> 2; matrix products, arithmetic and copies ran while one was open for 8% -> 5% of each run, Pallas kernels for 0% -> 7%
where the time goes in v2:
time: 114 us
  Pallas kernels  40.8 us (36%)
  blocking collectives  35 us (31%)
  starting transfers between devices  21.1 us (19%)
  waiting for transfers between devices  6.17 us (5%)
  other arithmetic  4.29 us (4%)
  local copies, waits for them, and re-layouts  3.65 us (3%)
  between operations  2.71 us (2%)
    all_to_all x1, blocking collectives, body(): lax.all_to_all(collect(held, pages), 'pool', split_axis=0, concat_axis=0,...  35 us
    pallas_call x1, Pallas kernels, attend(): pl.pallas_call(functools.partial(attend_kernel, pages, sub, chunk), grid=...  23.1 us
    all_to_all x1, starting transfers between devices, body(): lax.all_to_all(outgoing, 'pool', split_axis=0, concat_axis=0, tiled=True)  16.3 us
    pallas_call x1, Pallas kernels, attend_fresh(): pl.pallas_call(functools.partial(fresh_kernel, sub), grid=(count // block...  8.51 us
    pallas_call x1, Pallas kernels, collect(): pl.pallas_call(functools.partial(collect_kernel, pages, 4), in_specs=[pl....  5.26 us
    all_to_all x1, waiting for transfers between devices, body(): lax.all_to_all(outgoing, 'pool', split_axis=0, concat_axis=0, tiled=True)  5.18 us
    ppermute x1, starting transfers between devices, body(): peer = lax.ppermute(own, 'pd', [(0, 1), (1, 0)])  4.8 us
    concatenate x1, other arithmetic, body(): jnp.concatenate([q_latent, q_rope.reshape(stretch, heads, rope), mark], a...  4.28 us
  transfers between devices with their start and end apart: 2, of which 2 were waited for; matrix products, arithmetic and copies ran while one was open for 5% of the time, Pallas kernels for 7%

profile of v2, /device:TPU:1, one launch (start us, length us, event | category | flops | bytes accessed | tf_op | source)
XLA Modules:
  0.0 113.8 jit_solution(18049117909183165289)
XLA Ops:
  0.6 0.0 copy-start.3
  1.3 3.9 %shard_map.113 = bf16[4,32,24,128]{3,2,1,0:T(8,128)(2,1)} custom-call(s32[1]{0:T(128)S(6)} %copy.13.partner_ref, bf16[16,64,576]{2,1,0:T(8,128)(2,1)} %pages_ref.1, bf16[64,576]{1,0:T(8,128)(2,1)} %new_ref.3, s32[1,24]{1,0:T(1,128)} %owner_ref.1, s32[1,24]{1,0:T(1,128)} %slot_ref.1), custom_call_target="tpu_custom_call" | custom-call | flops 1000000000 | bytes 1500000 | tf_op jit(solution)/shard_map/pallas_call | solution.py:85
  5.3 16.3 %all-to-all-start = ((bf16[128,24,128]{2,1,0:T(8,128)(2,1)}), bf16[128,24,128]{2,1,0:T(8,128)(2,1)S(1)}, u32[]{:S(2)}, u32[]{:S(2)}) async-start(bf16[128,24,128]{2,1,0:T(8,128)(2,1)} %bitcast.6), calls=%async_computation | async-start | bytes 1572864 | tf_op jit(solution)/shard_map/all_to_all | solution.py:359
  21.6 0.0 copy-done.3
  21.6 1.1 concatenate.11
  22.8 0.1 broadcast_in_dim.2
  22.9 0.0 copy-start.2
  22.9 4.3 %pad_maximum_fusion.q_ref = bf16[4096,640]{1,0:T(8,128)(2,1)S(1)} fusion(bf16[4096,64]{1,0:T(8,128)(2,1)S(1)} %bitcast.5, bf16[4096,64]{1,0:T(8,128)(2,1)S(1)} %concatenate.11, bf16[4096,512]{1,0:T(8,128)(2,1)} %bitcast.4), kind=kLoop, calls=%fused_computation | loop fusion | flops 15728640 | bytes 10485760 | tf_op jit(solution)/shard_map/concatenate | solution.py:365
  27.2 0.0 copy-done.2
  27.2 8.5 %shard_map.114 = (f32[4096,512]{1,0:T(8,128)}, f32[4096,128]{1,0:T(8,128)S(1)}) custom-call(bf16[4096,640]{1,0:T(8,128)(2,1)S(1)} %pad_maximum_fusion.q_ref, bf16[64,576]{1,0:T(8,128)(2,1)S(1)} %copy-done.2), custom_call_target="tpu_custom_call" | custom-call | flops 5000000000 | bytes 16000000 | tf_op jit(solution)/shard_map/pallas_call | solution.py:195
  35.7 0.0 copy-start
  35.7 2.4 %copy-done = bf16[4096,640]{1,0:T(8,128)(2,1)} copy-done((bf16[4096,640]{1,0:T(8,128)(2,1)}, bf16[4096,640]{1,0:T(8,128)(2,1)S(1)}, u32[]{:S(2)}) %copy-start) | copy-done | bytes 5242904
  38.1 5.2 %all-to-all-done.all_ref = bf16[128,24,128]{2,1,0:T(8,128)(2,1)S(1)} async-done(((bf16[128,24,128]{2,1,0:T(8,128)(2,1)}), bf16[128,24,128]{2,1,0:T(8,128)(2,1)S(1)}, u32[]{:S(2)}, u32[]{:S(2)}) %all-to-all-start) | async-done | bytes 786464 | tf_op jit(solution)/shard_map/all_to_all | solution.py:359
  43.3 0.0 copy-start.1
  43.3 5.3 %shard_map.115 = bf16[128,32,128]{2,1,0:T(8,128)(2,1)S(1)} custom-call(bf16[128,24,128]{2,1,0:T(8,128)(2,1)S(1)} %all-to-all-done.all_ref), custom_call_target="tpu_custom_call" | custom-call | flops 4000000000 | bytes 1500000 | tf_op jit(solution)/shard_map/pallas_call | solution.py:149
  48.6 35.0 %all_to_all.10.own_ref = bf16[128,32,128]{2,1,0:T(8,128)(2,1)S(1)} all-to-all(bf16[128,32,128]{2,1,0:T(8,128)(2,1)S(1)} %shard_map.115), channel_id=1, replica_groups=mesh['pool'=128,'pd'=2] {'pool'}, dimensions={0} | all-to-all | bytes 2097152 | tf_op jit(solution)/shard_map/all_to_all | solution.py:371
  83.6 4.8 %collective-permute-start = (bf16[128,32,128]{2,1,0:T(8,128)(2,1)S(1)}, bf16[128,32,128]{2,1,0:T(8,128)(2,1)S(1)}, u32[]{:S(2)}, u32[]{:S(2)}) collective-permute-start(bf16[128,32,128]{2,1,0:T(8,128)(2,1)S(1)} %all_to_all.10.own_ref), channel_id=1, source_target_pairs={{0,1},{1,0},{2,3},{3,2},{4,5},{5,4},{6,7},{7,6},{8,9},{9,8},{10,11... | collective-permute-start | bytes 3145736 | tf_op jit(solution)/shard_map/ppermute | solution.py:372
  89.7 1.0 collective-permute-done.peer_ref
  90.7 0.0 copy-done.1
  90.7 23.1 %shard_map.116 = (bf16[4096,512]{1,0:T(8,128)(2,1)}, bf16[8,64,576]{2,1,0:T(8,128)(2,1)}) custom-call(s32[1]{0:T(128)S(6)} %copy.12.length_ref, s32[1]{0:T(128)S(6)} %copy.14.dest_ref, bf16[4096,640]{1,0:T(8,128)(2,1)} %copy-done, bf16[128,32,128]{2,1,0:T(8,128)(2,1)S(1)} %all_to_all.10.own_ref, bf16[128,32,128]{2,1,0:T(8,128)(2,1)S(1)} %collective-permute-done.peer_ref, ...), custom_call_target="tpu_custom_call" | custom-call | flops 14495514624 | bytes 20000000 | tf_op jit(solution)/shard_map/pallas_call | solution.py:322
  (1 shorter events, 0.0 us)
Async XLA Ops:
  0.6 21.0 %copy-start.3 = (bf16[64,4096]{1,0:T(8,128)(2,1)S(1)}, bf16[64,4096]{1,0:T(8,128)(2,1)}, u32[]{:S(2)}) copy-start(bf16[64,4096]{1,0:T(8,128)(2,1)} %param.11) | copy-start | bytes 1572868
  5.3 38.0 %all-to-all-start = ((bf16[128,24,128]{2,1,0:T(8,128)(2,1)}), bf16[128,24,128]{2,1,0:T(8,128)(2,1)S(1)}, u32[]{:S(2)}, u32[]{:S(2)}) async-start(bf16[128,24,128]{2,1,0:T(8,128)(2,1)} %bitcast.6), calls=%async_computation | async-start | bytes 1572864 | tf_op jit(solution)/shard_map/all_to_all | solution.py:359
  22.9 4.3 %copy-start.2 = (bf16[64,576]{1,0:T(8,128)(2,1)S(1)}, bf16[64,576]{1,0:T(8,128)(2,1)}, u32[]{:S(2)}) copy-start(bf16[64,576]{1,0:T(8,128)(2,1)} %new_ref.3) | copy-start | bytes 221188
  35.7 2.4 %copy-start = (bf16[4096,640]{1,0:T(8,128)(2,1)}, bf16[4096,640]{1,0:T(8,128)(2,1)S(1)}, u32[]{:S(2)}) copy-start(bf16[4096,640]{1,0:T(8,128)(2,1)S(1)} %pad_maximum_fusion.q_ref) | copy-start | bytes 15728644
  43.3 47.4 %copy-start.1 = (bf16[8,64,576]{2,1,0:T(8,128)(2,1)S(1)}, bf16[8,64,576]{2,1,0:T(8,128)(2,1)}, u32[]{:S(2)}) copy-start(bf16[8,64,576]{2,1,0:T(8,128)(2,1)} %cache_ref.1) | copy-start | bytes 1769476
  83.6 7.1 %collective-permute-start = (bf16[128,32,128]{2,1,0:T(8,128)(2,1)S(1)}, bf16[128,32,128]{2,1,0:T(8,128)(2,1)S(1)}, u32[]{:S(2)}, u32[]{:S(2)}) collective-permute-start(bf16[128,32,128]{2,1,0:T(8,128)(2,1)S(1)} %all_to_all.10.own_ref), channel_id=1, source_target_pairs={{0,1},{1,0},{2,3},{3,2},{4,5},{5,4},{6,7},{7,6},{8,9},{9,8},{10,11... | collective-permute-start | bytes 3145736 | tf_op jit(solution)/shard_map/ppermute | solution.py:372

commit v3 on v2

--- a/solution.py
+++ b/solution.py
@@ -13,6 +13,8 @@
 lanes = 128
 f32 = jnp.float32
 bf16 = jnp.bfloat16
+exchange_rows = 20
+reply_rows = 30
 
 
 def iota(shape, axis):
@@ -36,12 +38,11 @@
 
 
 def spread_kernel(partner_ref, pages_ref, new_ref, owner_ref, slot_ref, out_ref):
-    slots = pages_ref.shape[0]
-    rows = out_ref.shape[1]
-    begin = pl.multiple_of(lax.axis_index("pd") * (2 * rows) + pl.program_id(0) * rows, rows)
-    held = 24
-    pages = pages_ref[:, pl.ds(begin, rows), :].reshape(slots * rows, pages_ref.shape[2])
-    fresh = new_ref[pl.ds(begin, rows), :]
+    slots, _, _, rows, width = pages_ref.shape
+    core = lax.axis_index("pd")
+    held = exchange_rows
+    pages = pages_ref[:, core, 0].reshape(slots * rows, width)
+    fresh = new_ref[core, 0]
     latent = 4 * lanes
     total = rows * held
     out_row = iota((total, 1), 0)
@@ -63,19 +64,21 @@
     slot = iota((slots * rows, latent), 0) // rows
     rope = mm(pages[:, latent:], tile)
     rope = jnp.where(group == slot % 8, rope, 0.0).astype(bf16)
-    new_rope = mm(fresh[:, latent:], tile).astype(bf16)
+    first = iota((rows, latent), 1) % lanes < 16
+    new_rope = jnp.where(first, mm(fresh[:, latent:], tile), 0.0).astype(bf16)
     result = mm(take_latent, pages[:, :latent]) + mm(take_rope, rope)
     result += mm(take_new, fresh[:, :latent]) + mm(take_new_rope, new_rope)
     asked = owner_ref.shape[1]
     lane = iota((asked, lanes), 1)
     at = iota((asked, lanes), 0)
-    meta = mm(owner_ref[...].astype(f32).astype(bf16), picks(lane == at))
-    meta += mm(slot_ref[...].astype(f32).astype(bf16), picks(lane == at + 32))
-    meta = jnp.where(iota((1, lanes), 1) == 64, partner_ref[0].astype(f32), meta)
+    meta = mm(owner_ref[...].astype(f32).astype(bf16), picks(lane == at + 32))
+    meta += mm(slot_ref[...].astype(f32).astype(bf16), picks(lane == at + 64))
+    meta = jnp.where(iota((1, lanes), 1) == 96, partner_ref[0].astype(f32), meta)
     for quarter in range(4):
         part = result[:, quarter * lanes : (quarter + 1) * lanes]
-        part = jnp.where(out_k == 20, meta, part)
-        out_ref[quarter] = part.reshape(rows, held, lanes).astype(bf16)
+        part = jnp.where(out_k == 19, part + meta, part)
+        begin = pl.multiple_of(quarter * 2 * total + pl.program_id(0) * total, total)
+        out_ref[pl.ds(begin, total), :] = part.astype(bf16)
 
 
 def spread(partner, pages, fresh, owner, slot):
@@ -87,24 +90,25 @@
         grid=(2,),
         in_specs=[
             pl.BlockSpec(memory_space=pltpu.SMEM),
-            whole(pages),
-            whole(fresh),
+            pl.BlockSpec((slots, 2, 1, rows, width), lambda i: (0, 0, i, 0, 0)),
+            pl.BlockSpec((2, 1, rows, width), lambda i: (0, i, 0, 0)),
             whole(owner),
             whole(slot),
         ],
-        out_specs=pl.BlockSpec((4, rows, 24, lanes), lambda i: (0, i, 0, 0)),
-        out_shape=jax.ShapeDtypeStruct((4, 2 * rows, 24, lanes), bf16),
+        out_specs=pl.BlockSpec(memory_space=pltpu.VMEM),
+        out_shape=jax.ShapeDtypeStruct((8 * rows * exchange_rows, lanes), bf16),
         compiler_params=pltpu.CompilerParams(vmem_limit_bytes=60 * 1024 * 1024),
         cost_estimate=pl.CostEstimate(flops=10**9, bytes_accessed=1_500_000, transcendentals=0),
-    )(partner, pages, fresh, owner, slot)
-    return out.reshape(8 * rows, 24, lanes)
+    )(partner, pages.reshape(slots, 2, 2, rows, width), fresh.reshape(2, 2, rows, width), owner, slot)
+    return out.reshape(8 * rows, exchange_rows // 2, 2, lanes)
 
 
 def collect_kernel(pages, group, all_ref, out_ref, rows_ref, table_ref, stage_ref):
-    owners, held, _ = all_ref.shape
+    held = exchange_rows
+    owners = all_ref.shape[0] // held
     slots = 16
-    size = 32
-    rows_ref[...] = all_ref[...].astype(f32).reshape(owners * held, lanes)
+    size = reply_rows
+    rows_ref[...] = all_ref[...].astype(f32)
     src = iota((lanes, lanes), 0)
     dst = iota((lanes, lanes), 1)
     tile = picks(src % 16 == dst % 16)
@@ -115,14 +119,14 @@
         piece = rows_ref[pl.ds(17 + slot // 8, owners, stride=held), :]
         piece = jnp.where(lane // 16 == slot % 8, piece, 0.0).astype(bf16)
         table_ref[at, lanes:] = mm(piece, tile).astype(bf16)
-    meta = rows_ref[pl.ds(20, owners, stride=held), :]
+    meta = rows_ref[pl.ds(19, owners, stride=held), :]
     blank = jnp.zeros((owners, lanes), f32)
     ropes = [blank] * (pages // 8)
     for start in range(0, pages, group):
         wanted = []
         for place in range(start, start + group):
-            owner = picks(meta[:, place : place + 1] == lane.astype(f32))
-            slot = jnp.broadcast_to(meta[:, 32 + place : 33 + place], (owners, lanes)).astype(bf16)
+            owner = picks(meta[:, 32 + place : 33 + place] == lane.astype(f32))
+            slot = jnp.broadcast_to(meta[:, 64 + place : 65 + place], (owners, lanes)).astype(bf16)
             wanted.append(
                 jnp.concatenate(
                     [jnp.where(slot == jnp.bfloat16(k), owner, jnp.bfloat16(0)) for k in range(slots)], axis=1
@@ -134,31 +138,33 @@
             got = found[k * owners : (k + 1) * owners]
             stage_ref[pl.ds(place, owners, stride=size), :] = got[:, :lanes]
             ropes[place // 8] += jnp.where(lane // 16 == place % 8, got[:, lanes:], 0.0)
-    comes = picks(meta[:, 64:65].astype(jnp.int32) == lane)
+    comes = picks(meta[:, 96:97].astype(jnp.int32) == lane)
     arriving = mm_first(comes, rows_ref[pl.ds(16, owners, stride=held), :].astype(bf16))
-    arriving_rope = mm_first(comes, rows_ref[pl.ds(19, owners, stride=held), :].astype(bf16))
+    arriving_rope = mm_first(comes, jnp.where(lane < 16, meta, 0.0).astype(bf16))
     tail = [arriving] + ropes + [arriving_rope]
     tail += [blank] * (size - pages - len(tail))
     for k, piece in enumerate(tail):
         stage_ref[pl.ds(pages + k, owners, stride=size), :] = piece
-    out_ref[...] = stage_ref[...].reshape(owners, size, lanes).astype(bf16)
+    out_ref[...] = stage_ref[...].astype(bf16)
 
 
 def collect(held, pages):
     owners = held.shape[0]
-    return pl.pallas_call(
+    held = held.reshape(owners * exchange_rows, lanes)
+    out = pl.pallas_call(
         functools.partial(collect_kernel, pages, 4),
         in_specs=[pl.BlockSpec(memory_space=pltpu.VMEM)],
         out_specs=pl.BlockSpec(memory_space=pltpu.VMEM),
-        out_shape=jax.ShapeDtypeStruct((owners, 32, lanes), bf16),
+        out_shape=jax.ShapeDtypeStruct((owners * reply_rows, lanes), bf16),
         scratch_shapes=[
-            pltpu.VMEM((owners * held.shape[1], lanes), f32),
+            pltpu.VMEM(held.shape, f32),
             pltpu.VMEM((owners * 16, 2 * lanes), bf16),
-            pltpu.VMEM((owners * 32, lanes), f32),
+            pltpu.VMEM((owners * reply_rows, lanes), f32),
         ],
         compiler_params=pltpu.CompilerParams(vmem_limit_bytes=40 * 1024 * 1024),
         cost_estimate=pl.CostEstimate(flops=4 * 10**9, bytes_accessed=1_500_000, transcendentals=0),
     )(held)
+    return out.reshape(owners, reply_rows // 2, 2, lanes)
 
 
 factor = score_scale * log2_e
@@ -230,9 +236,11 @@
     key_ref,
     score_ref,
     arrive_ref,
+    rows_ref,
 ):
     latent = 4 * lanes
-    rows = own_ref.shape[0] // 4
+    size = reply_rows
+    rows = own_ref.shape[0] // (4 * size)
     half = rows * pages
     keys = 2 * half
     step = pl.program_id(0)
@@ -242,26 +250,28 @@
         core = lax.axis_index("pd")
         src = iota((lanes, lanes), 0)
         dst = iota((lanes, lanes), 1)
-        group = iota((8, lanes), 1) // 16 == iota((8, lanes), 0)
+        lane = iota((rows, lanes), 1)
         key = iota((half, 1), 0)
-        row = key // pages
-        place = (key - row * pages) * 64 + row
+        place = (key // rows) * 64 + key % rows
         for side, ref in enumerate((own_ref, peer_ref)):
             at = slice(side * half, (side + 1) * half)
             spot = pl.multiple_of((core if side == 0 else 1 - core) * rows, rows)
             rope_keys = jnp.zeros((half, lanes), f32)
             arrived_rope = jnp.zeros((rows, lanes), f32)
+            rows_ref[...] = ref[...].astype(f32)
             for quarter in range(4):
                 cols = slice(quarter * lanes, (quarter + 1) * lanes)
-                block = ref[quarter * rows : (quarter + 1) * rows].astype(f32)
-                key_ref[at, cols] = block[:, :pages].reshape(half, lanes).astype(bf16)
-                tail = block[:, pages:]
-                pieces = [jnp.where(group[None], tail[:, 1 + k : 2 + k], 0.0) for k in range(pages // 8)]
-                rope = jnp.concatenate(pieces, axis=1).reshape(half, lanes).astype(bf16)
+                take = lambda k: rows_ref[pl.ds(quarter * rows * size + k, rows, stride=size), :]
+                for k in range(pages):
+                    begin = side * half + k * rows
+                    key_ref[begin : begin + rows, cols] = take(k).astype(bf16)
+                ropes = [take(pages + 1 + k) for k in range(pages // 8)]
+                pieces = [jnp.where(lane // 16 == k % 8, ropes[k // 8], 0.0) for k in range(pages)]
+                rope = jnp.concatenate(pieces, axis=0).astype(bf16)
                 put = picks((dst // 16 == quarter) & (dst % 16 == src % 16))
                 rope_keys += mm(rope, put)
-                arrive_ref[pl.ds(spot, rows), cols] = tail[:, 0, :]
-                last = jnp.where(iota((rows, lanes), 1) < 16, tail[:, 1 + pages // 8, :], 0.0)
+                arrive_ref[pl.ds(spot, rows), cols] = take(pages)
+                last = jnp.where(lane < 16, take(pages + 1 + pages // 8), 0.0)
                 arrived_rope += mm(last.astype(bf16), put)
             arrive_ref[pl.ds(spot, rows), latent:] = arrived_rope[:, :64]
             bias = jnp.where(place + spot < length_ref[0], 0.0, hidden)
@@ -332,6 +342,7 @@
             pltpu.VMEM((keys, width), bf16),
             pltpu.VMEM((2, sub, keys), f32),
             pltpu.VMEM(cache.shape[1:], f32),
+            pltpu.VMEM(own.shape, f32),
         ],
         compiler_params=pltpu.CompilerParams(vmem_limit_bytes=48 * 1024 * 1024),
         cost_estimate=pl.CostEstimate(
@@ -369,6 +380,7 @@
 
     pages = page_owner.shape[1]
     own = lax.all_to_all(collect(held, pages), "pool", split_axis=0, concat_axis=0, tiled=True)
+    own = own.reshape(-1, lanes)
     peer = lax.ppermute(own, "pd", [(0, 1), (1, 0)])
     context, decode_out = attend(prefix_len, dest_slot, queries, own, peer, acc, stat, decode_cache, pages)
     return (context.reshape(stretch, heads, latent), decode_out)

time: 114 us -> 110 us (0.965)
  waiting for transfers between devices: 6.17 us -> 3.43 us
  Pallas kernels: 40.8 us -> 39.2 us
    all_to_all x1, waiting for transfers between devices: 5.18 us -> 2.53 us  [body(): lax.all_to_all(outgoing, 'pool', split_axis=0, concat_axis=0, tiled=True)]
    pallas_call x1, Pallas kernels: 5.26 us -> 3.78 us  [collect(): pl.pallas_call(functools.partial(collect_kernel, pages, 4), in_specs=[pl....]
  transfers between devices with their start and end apart: 2 -> 2, of which waited for: 2 -> 2; matrix products, arithmetic and copies ran while one was open for 5% -> 5% of each run, Pallas kernels for 7% -> 8%
where the time goes in v3:
time: 110 us
  Pallas kernels  39.2 us (36%)
  blocking collectives  35.8 us (33%)
  starting transfers between devices  20.7 us (19%)
  other arithmetic  4.29 us (4%)
  local copies, waits for them, and re-layouts  3.65 us (3%)
  waiting for transfers between devices  3.43 us (3%)
  between operations  2.71 us (2%)
    all_to_all x1, blocking collectives, body(): lax.all_to_all(collect(held, pages), 'pool', split_axis=0, concat_axis=0,...  35.8 us
    pallas_call x1, Pallas kernels, attend(): pl.pallas_call(functools.partial(attend_kernel, pages, sub, chunk), grid=...  23.2 us
    all_to_all x1, starting transfers between devices, body(): lax.all_to_all(outgoing, 'pool', split_axis=0, concat_axis=0, tiled=True)  16.3 us
    pallas_call x1, Pallas kernels, attend_fresh(): pl.pallas_call(functools.partial(fresh_kernel, sub), grid=(count // block...  8.51 us
    ppermute x1, starting transfers between devices, body(): peer = lax.ppermute(own, 'pd', [(0, 1), (1, 0)])  4.36 us
    concatenate x1, other arithmetic, body(): jnp.concatenate([q_latent, q_rope.reshape(stretch, heads, rope), mark], a...  4.28 us
    pallas_call x1, Pallas kernels, collect(): pl.pallas_call(functools.partial(collect_kernel, pages, 4), in_specs=[pl....  3.78 us
    pallas_call x1, Pallas kernels, spread(): pl.pallas_call(spread_kernel, grid=(2,), in_specs=[pl.BlockSpec(memory_sp...  3.74 us
  transfers between devices with their start and end apart: 2, of which 2 were waited for; matrix products, arithmetic and copies ran while one was open for 5% of the time, Pallas kernels for 8%

profile of v3, /device:TPU:1, one launch (start us, length us, event | category | flops | bytes accessed | tf_op | source)
XLA Modules:
  0.0 109.9 jit_solution(6432722873073457857)
XLA Ops:
  0.6 0.0 copy-start.3
  1.3 3.7 %shard_map.113 = bf16[2560,128]{1,0:T(8,128)(2,1)} custom-call(s32[1]{0:T(128)S(6)} %copy.13.partner_ref, bf16[16,2,2,16,576]{4,3,2,1,0:T(8,128)(2,1)} %bitcast.17, bf16[2,2,16,576]{3,2,1,0:T(8,128)(2,1)} %bitcast.13, s32[1,24]{1,0:T(1,128)} %owner_ref.1, s32[1,24]{1,0:T(1,128)} %slot_ref.1), custom_call_target="tpu_custom_call" | custom-call | flops 1000000000 | bytes 1500000 | tf_op jit(solution)/shard_map/pallas_call | solution.py:88
  5.1 16.3 %all-to-all-start = ((bf16[128,10,2,128]{3,2,1,0:T(2,128)(2,1)}), bf16[128,10,2,128]{3,2,1,0:T(2,128)(2,1)S(1)}, u32[]{:S(2)}, u32[]{:S(2)}) async-start(bf16[128,10,2,128]{3,2,1,0:T(2,128)(2,1)} %bitcast.16), calls=%async_computation | async-start | bytes 1310720 | tf_op jit(solution)/shard_map/all_to_all | solution.py:370
  21.4 0.0 copy-done.3
  21.4 1.1 %concatenate.11 = bf16[4096,64]{1,0:T(8,128)(2,1)S(1)} reshape(bf16[64,4096]{1,0:T(8,128)(2,1)S(1)} %copy-done.3) | data formatting | bytes 1048576 | tf_op jit(solution)/shard_map/concatenate | solution.py:376
  22.6 0.1 broadcast_in_dim.2
  22.7 0.0 copy-start.2
  22.7 4.3 %pad_maximum_fusion.q_ref = bf16[4096,640]{1,0:T(8,128)(2,1)S(1)} fusion(bf16[4096,64]{1,0:T(8,128)(2,1)S(1)} %bitcast.15, bf16[4096,64]{1,0:T(8,128)(2,1)S(1)} %concatenate.11, bf16[4096,512]{1,0:T(8,128)(2,1)} %bitcast.14), kind=kLoop, calls=%fused_computation | loop fusion | flops 15728640 | bytes 10485760 | tf_op jit(solution)/shard_map/concatenate | solution.py:376
  27.0 0.0 copy-done.2
  27.0 8.5 %shard_map.114 = (f32[4096,512]{1,0:T(8,128)}, f32[4096,128]{1,0:T(8,128)S(1)}) custom-call(bf16[4096,640]{1,0:T(8,128)(2,1)S(1)} %pad_maximum_fusion.q_ref, bf16[64,576]{1,0:T(8,128)(2,1)S(1)} %copy-done.2), custom_call_target="tpu_custom_call" | custom-call | flops 5000000000 | bytes 16000000 | tf_op jit(solution)/shard_map/pallas_call | solution.py:201
  35.6 0.0 copy-start
  35.6 2.4 %copy-done = bf16[4096,640]{1,0:T(8,128)(2,1)} copy-done((bf16[4096,640]{1,0:T(8,128)(2,1)}, bf16[4096,640]{1,0:T(8,128)(2,1)S(1)}, u32[]{:S(2)}) %copy-start) | copy-done | bytes 5242904
  37.9 2.5 %all-to-all-done = bf16[128,10,2,128]{3,2,1,0:T(2,128)(2,1)S(1)} async-done(((bf16[128,10,2,128]{3,2,1,0:T(2,128)(2,1)}), bf16[128,10,2,128]{3,2,1,0:T(2,128)(2,1)S(1)}, u32[]{:S(2)}, u32[]{:S(2)}) %all-to-all-start) | async-done | bytes 655392 | tf_op jit(solution)/shard_map/all_to_all | solution.py:370
  40.5 0.0 copy-start.1
  40.5 3.8 %shard_map.115 = bf16[3840,128]{1,0:T(8,128)(2,1)S(1)} custom-call(bf16[2560,128]{1,0:T(8,128)(2,1)S(1)} %bitcast.12), custom_call_target="tpu_custom_call" | custom-call | flops 4000000000 | bytes 1500000 | tf_op jit(solution)/shard_map/pallas_call | solution.py:154
  44.3 35.8 %all_to_all.10 = bf16[128,15,2,128]{3,2,1,0:T(2,128)(2,1)S(1)} all-to-all(bf16[128,15,2,128]{3,2,1,0:T(2,128)(2,1)S(1)} %bitcast.11), channel_id=1, replica_groups=mesh['pool'=128,'pd'=2] {'pool'}, dimensions={0} | all-to-all | bytes 1966080 | tf_op jit(solution)/shard_map/all_to_all | solution.py:382
  80.1 4.4 %collective-permute-start = (bf16[3840,128]{1,0:T(8,128)(2,1)S(1)}, bf16[3840,128]{1,0:T(8,128)(2,1)S(1)}, u32[]{:S(2)}, u32[]{:S(2)}) collective-permute-start(bf16[3840,128]{1,0:T(8,128)(2,1)S(1)} %bitcast.9), channel_id=1, source_target_pairs={{0,1},{1,0},{2,3},{3,2},{4,5},{5,4},{6,7},{7,6},{8,9},{9,8},{10,11... | collective-permute-start | bytes 2949128 | tf_op jit(solution)/shard_map/ppermute | solution.py:384
  85.7 0.9 collective-permute-done.peer_ref
  86.6 0.0 copy-done.1
  86.6 23.2 %shard_map.116 = (bf16[4096,512]{1,0:T(8,128)(2,1)}, bf16[8,64,576]{2,1,0:T(8,128)(2,1)}) custom-call(s32[1]{0:T(128)S(6)} %copy.12.length_ref, s32[1]{0:T(128)S(6)} %copy.14.dest_ref, bf16[4096,640]{1,0:T(8,128)(2,1)} %copy-done, bf16[3840,128]{1,0:T(8,128)(2,1)S(1)} %bitcast.10, bf16[3840,128]{1,0:T(8,128)(2,1)S(1)} %collective-permute-done.peer_ref, ...), custom_call_target="tpu_custom_call" | custom-call | flops 14495514624 | bytes 20000000 | tf_op jit(solution)/shard_map/pallas_call | solution.py:332
  (1 shorter events, 0.0 us)
Async XLA Ops:
  0.6 20.8 %copy-start.3 = (bf16[64,4096]{1,0:T(8,128)(2,1)S(1)}, bf16[64,4096]{1,0:T(8,128)(2,1)}, u32[]{:S(2)}) copy-start(bf16[64,4096]{1,0:T(8,128)(2,1)} %param.11) | copy-start | bytes 1572868
  5.1 35.4 %all-to-all-start = ((bf16[128,10,2,128]{3,2,1,0:T(2,128)(2,1)}), bf16[128,10,2,128]{3,2,1,0:T(2,128)(2,1)S(1)}, u32[]{:S(2)}, u32[]{:S(2)}) async-start(bf16[128,10,2,128]{3,2,1,0:T(2,128)(2,1)} %bitcast.16), calls=%async_computation | async-start | bytes 1310720 | tf_op jit(solution)/shard_map/all_to_all | solution.py:370
  22.7 4.3 %copy-start.2 = (bf16[64,576]{1,0:T(8,128)(2,1)S(1)}, bf16[64,576]{1,0:T(8,128)(2,1)}, u32[]{:S(2)}) copy-start(bf16[64,576]{1,0:T(8,128)(2,1)} %new_ref.1) | copy-start | bytes 221188
  35.6 2.4 %copy-start = (bf16[4096,640]{1,0:T(8,128)(2,1)}, bf16[4096,640]{1,0:T(8,128)(2,1)S(1)}, u32[]{:S(2)}) copy-start(bf16[4096,640]{1,0:T(8,128)(2,1)S(1)} %pad_maximum_fusion.q_ref) | copy-start | bytes 15728644
  40.5 46.2 %copy-start.1 = (bf16[8,64,576]{2,1,0:T(8,128)(2,1)S(1)}, bf16[8,64,576]{2,1,0:T(8,128)(2,1)}, u32[]{:S(2)}) copy-start(bf16[8,64,576]{2,1,0:T(8,128)(2,1)} %cache_ref.1) | copy-start | bytes 1769476
  80.1 6.6 %collective-permute-start = (bf16[3840,128]{1,0:T(8,128)(2,1)S(1)}, bf16[3840,128]{1,0:T(8,128)(2,1)S(1)}, u32[]{:S(2)}, u32[]{:S(2)}) collective-permute-start(bf16[3840,128]{1,0:T(8,128)(2,1)S(1)} %bitcast.9), channel_id=1, source_target_pairs={{0,1},{1,0},{2,3},{3,2},{4,5},{5,4},{6,7},{7,6},{8,9},{9,8},{10,11... | collective-permute-start | bytes 2949128 | tf_op jit(solution)/shard_map/ppermute | solution.py:384

commit v4 on v3

--- a/solution.py
+++ b/solution.py
@@ -46,25 +46,26 @@
     latent = 4 * lanes
     total = rows * held
     out_row = iota((total, 1), 0)
-    out_r = out_row // held
-    out_k = out_row % held
+    out_r = (out_row * 3277) >> 16
+    out_k = out_row - out_r * held
     in_row = iota((total, slots * rows), 1)
-    in_r = in_row % rows
-    in_s = in_row // rows
+    shift = rows.bit_length() - 1
+    in_r = in_row & (rows - 1)
+    in_s = in_row >> shift
     same = in_r == out_r
     take_latent = picks(same & (in_s == out_k))
-    take_rope = picks(same & (in_s // 8 == out_k - 17))
+    take_rope = picks(same & ((in_s >> 3) == out_k - 17))
     new_same = iota((total, rows), 1) == out_r
     take_new = picks(new_same & (out_k == 16))
     take_new_rope = picks(new_same & (out_k == 19))
     src = iota((64, latent), 0)
     dst = iota((64, latent), 1)
-    tile = picks((src // 16 == dst // lanes) & (src % 16 == dst % 16))
-    group = (iota((slots * rows, latent), 1) % lanes) // 16
-    slot = iota((slots * rows, latent), 0) // rows
+    tile = picks(((src >> 4) == (dst >> 7)) & ((src & 15) == (dst & 15)))
+    group = (iota((slots * rows, latent), 1) >> 4) & 7
+    slot = iota((slots * rows, latent), 0) >> shift
     rope = mm(pages[:, latent:], tile)
-    rope = jnp.where(group == slot % 8, rope, 0.0).astype(bf16)
-    first = iota((rows, latent), 1) % lanes < 16
+    rope = jnp.where(group == (slot & 7), rope, 0.0).astype(bf16)
+    first = (iota((rows, latent), 1) & (lanes - 1)) < 16
     new_rope = jnp.where(first, mm(fresh[:, latent:], tile), 0.0).astype(bf16)
     result = mm(take_latent, pages[:, :latent]) + mm(take_rope, rope)
     result += mm(take_new, fresh[:, :latent]) + mm(take_new_rope, new_rope)
@@ -111,13 +112,13 @@
     rows_ref[...] = all_ref[...].astype(f32)
     src = iota((lanes, lanes), 0)
     dst = iota((lanes, lanes), 1)
-    tile = picks(src % 16 == dst % 16)
+    tile = picks((src & 15) == (dst & 15))
     lane = iota((owners, lanes), 1)
     for slot in range(slots):
         at = slice(slot * owners, (slot + 1) * owners)
         table_ref[at, :lanes] = rows_ref[pl.ds(slot, owners, stride=held), :].astype(bf16)
         piece = rows_ref[pl.ds(17 + slot // 8, owners, stride=held), :]
-        piece = jnp.where(lane // 16 == slot % 8, piece, 0.0).astype(bf16)
+        piece = jnp.where((lane >> 4) == slot % 8, piece, 0.0).astype(bf16)
         table_ref[at, lanes:] = mm(piece, tile).astype(bf16)
     meta = rows_ref[pl.ds(19, owners, stride=held), :]
     blank = jnp.zeros((owners, lanes), f32)
@@ -137,7 +138,7 @@
             place = start + k
             got = found[k * owners : (k + 1) * owners]
             stage_ref[pl.ds(place, owners, stride=size), :] = got[:, :lanes]
-            ropes[place // 8] += jnp.where(lane // 16 == place % 8, got[:, lanes:], 0.0)
+            ropes[place // 8] += jnp.where((lane >> 4) == place % 8, got[:, lanes:], 0.0)
     comes = picks(meta[:, 96:97].astype(jnp.int32) == lane)
     arriving = mm_first(comes, rows_ref[pl.ds(16, owners, stride=held), :].astype(bf16))
     arriving_rope = mm_first(comes, jnp.where(lane < 16, meta, 0.0).astype(bf16))
@@ -170,7 +171,11 @@
 factor = score_scale * log2_e
 
 
-def fresh_kernel(sub, q_ref, new_ref, acc_ref, stat_ref, value_ref, key_ref):
+def joined(latent_ref, rope_ref, at):
+    return jnp.concatenate([latent_ref[at, :], rope_ref[at, :]], axis=1)
+
+
+def fresh_kernel(sub, q_ref, rope_ref, new_ref, acc_ref, stat_ref, value_ref, key_ref):
     latent = 4 * lanes
 
     @pl.when(pl.program_id(0) == 0)
@@ -187,7 +192,7 @@
 
     for part in range(q_ref.shape[0] // sub):
         at = slice(part * sub, (part + 1) * sub)
-        scores = mm(q_ref[at, :], key_ref[...])
+        scores = mm(joined(q_ref, rope_ref, at), key_ref[...])
         top = jnp.max(scores, axis=1, keepdims=True)
         weight = jnp.exp2((scores - top) * jnp.float32(factor))
         total = jnp.sum(weight, axis=1, keepdims=True)
@@ -195,14 +200,15 @@
         stat_ref[at, :] = jnp.where(iota((sub, lanes), 1) < 64, top, total)
 
 
-def attend_fresh(queries, fresh, block=512, sub=256):
-    count, width = queries.shape
-    latent = 4 * lanes
+def attend_fresh(queries, ropes, fresh, block=1024, sub=256):
+    count, latent = queries.shape
+    width = latent + lanes
     return pl.pallas_call(
         functools.partial(fresh_kernel, sub),
         grid=(count // block,),
         in_specs=[
-            pl.BlockSpec((block, width), lambda i: (i, 0)),
+            pl.BlockSpec((block, latent), lambda i: (i, 0)),
+            pl.BlockSpec((block, lanes), lambda i: (i, 0)),
             pl.BlockSpec(fresh.shape, lambda i: (0, 0)),
         ],
         out_specs=[
@@ -216,7 +222,62 @@
         scratch_shapes=[pltpu.VMEM((lanes, latent), bf16), pltpu.VMEM((width, lanes), bf16)],
         compiler_params=pltpu.CompilerParams(vmem_limit_bytes=40 * 1024 * 1024),
         cost_estimate=pl.CostEstimate(flops=5 * 10**9, bytes_accessed=16_000_000, transcendentals=count * lanes),
-    )(queries, fresh)
+    )(queries, ropes, fresh)
+
+
+def unpack(pages, spot, length, ref, rows_ref, key_ref, arrive_ref):
+    latent = 4 * lanes
+    size = reply_rows
+    rows = ref.shape[0] // (4 * size)
+    half = rows * pages
+    shift = rows.bit_length() - 1
+    src = iota((lanes, lanes), 0)
+    dst = iota((lanes, lanes), 1)
+    lane = iota((rows, lanes), 1)
+    rope_keys = jnp.zeros((half, lanes), f32)
+    arrived_rope = jnp.zeros((rows, lanes), f32)
+    rows_ref[...] = ref[...].astype(f32)
+    for quarter in range(4):
+        cols = slice(quarter * lanes, (quarter + 1) * lanes)
+        take = lambda k: rows_ref[pl.ds(quarter * rows * size + k, rows, stride=size), :]
+        for k in range(pages):
+            key_ref[k * rows : (k + 1) * rows, cols] = take(k).astype(bf16)
+        ropes = [take(pages + 1 + k) for k in range(pages // 8)]
+        pieces = [jnp.where((lane >> 4) == k % 8, ropes[k // 8], 0.0) for k in range(pages)]
+        rope = jnp.concatenate(pieces, axis=0).astype(bf16)
+        put = picks(((dst >> 4) == quarter) & ((dst & 15) == (src & 15)))
+        rope_keys += mm(rope, put)
+        arrive_ref[:, cols] = take(pages)
+        last = jnp.where(lane < 16, take(pages + 1 + pages // 8), 0.0)
+        arrived_rope += mm(last.astype(bf16), put)
+    arrive_ref[:, latent:] = arrived_rope[:, :64]
+    key = iota((half, lanes), 0)
+    place = (key >> shift) * 64 + (key & (rows - 1)) + spot
+    bias = jnp.where(place < length, 0.0, hidden)
+    extra = jnp.where(iota((half, lanes), 1) < 64, rope_keys, bias)
+    key_ref[:, latent:] = extra.astype(bf16)
+
+
+def unpack_kernel(pages, length_ref, own_ref, key_ref, arrive_ref, rows_ref):
+    spot = lax.axis_index("pd") * (own_ref.shape[0] // (4 * reply_rows))
+    unpack(pages, spot, length_ref[0], own_ref, rows_ref, key_ref, arrive_ref)
+
+
+def unpack_own(length, own, pages, width):
+    rows = own.shape[0] // (4 * reply_rows)
+    inside = pl.BlockSpec(memory_space=pltpu.VMEM)
+    return pl.pallas_call(
+        functools.partial(unpack_kernel, pages),
+        in_specs=[pl.BlockSpec(memory_space=pltpu.SMEM), inside],
+        out_specs=[inside, inside],
+        out_shape=[
+            jax.ShapeDtypeStruct((rows * pages, 5 * lanes), bf16),
+            jax.ShapeDtypeStruct((rows, width), f32),
+        ],
+        scratch_shapes=[pltpu.VMEM(own.shape, f32)],
+        compiler_params=pltpu.CompilerParams(vmem_limit_bytes=40 * 1024 * 1024),
+        cost_estimate=pl.CostEstimate(flops=10**9, bytes_accessed=2_000_000, transcendentals=0),
+    )(length, own)
 
 
 def attend_kernel(
@@ -226,7 +287,9 @@
     length_ref,
     dest_ref,
     q_ref,
+    rope_ref,
     own_ref,
+    mine_ref,
     peer_ref,
     acc_ref,
     stat_ref,
@@ -239,53 +302,32 @@
     rows_ref,
 ):
     latent = 4 * lanes
-    size = reply_rows
-    rows = own_ref.shape[0] // (4 * size)
+    rows = mine_ref.shape[0]
     half = rows * pages
     keys = 2 * half
     step = pl.program_id(0)
 
+    def key_block(begin, cols):
+        ref, at = (own_ref, begin) if begin < half else (key_ref, begin - half)
+        return ref[at : at + chunk, cols]
+
     @pl.when(step == 0)
     def build():
         core = lax.axis_index("pd")
-        src = iota((lanes, lanes), 0)
-        dst = iota((lanes, lanes), 1)
-        lane = iota((rows, lanes), 1)
-        key = iota((half, 1), 0)
-        place = (key // rows) * 64 + key % rows
-        for side, ref in enumerate((own_ref, peer_ref)):
-            at = slice(side * half, (side + 1) * half)
-            spot = pl.multiple_of((core if side == 0 else 1 - core) * rows, rows)
-            rope_keys = jnp.zeros((half, lanes), f32)
-            arrived_rope = jnp.zeros((rows, lanes), f32)
-            rows_ref[...] = ref[...].astype(f32)
-            for quarter in range(4):
-                cols = slice(quarter * lanes, (quarter + 1) * lanes)
-                take = lambda k: rows_ref[pl.ds(quarter * rows * size + k, rows, stride=size), :]
-                for k in range(pages):
-                    begin = side * half + k * rows
-                    key_ref[begin : begin + rows, cols] = take(k).astype(bf16)
-                ropes = [take(pages + 1 + k) for k in range(pages // 8)]
-                pieces = [jnp.where(lane // 16 == k % 8, ropes[k // 8], 0.0) for k in range(pages)]
-                rope = jnp.concatenate(pieces, axis=0).astype(bf16)
-                put = picks((dst // 16 == quarter) & (dst % 16 == src % 16))
-                rope_keys += mm(rope, put)
-                arrive_ref[pl.ds(spot, rows), cols] = take(pages)
-                last = jnp.where(lane < 16, take(pages + 1 + pages // 8), 0.0)
-                arrived_rope += mm(last.astype(bf16), put)
-            arrive_ref[pl.ds(spot, rows), latent:] = arrived_rope[:, :64]
-            bias = jnp.where(place + spot < length_ref[0], 0.0, hidden)
-            joined = jnp.where(iota((half, lanes), 1) < 64, rope_keys, bias)
-            key_ref[at, latent:] = joined.astype(bf16)
+        spot = pl.multiple_of(core * rows, rows)
+        other = pl.multiple_of((1 - core) * rows, rows)
+        arrive_ref[pl.ds(spot, rows), :] = mine_ref[...]
+        unpack(pages, other, length_ref[0], peer_ref, rows_ref, key_ref, arrive_ref.at[pl.ds(other, rows), :])
 
     count = q_ref.shape[0] // sub
     scale = jnp.float32(factor)
 
     def score(part):
         at = slice(part * sub, (part + 1) * sub)
+        query = joined(q_ref, rope_ref, at)
         top = None
         for begin in range(0, keys, chunk):
-            found = mm_last(q_ref[at, :], key_ref[begin : begin + chunk, :])
+            found = mm_last(query, key_block(begin, slice(None)))
             score_ref[part % 2, :, begin : begin + chunk] = found
             for k in range(0, chunk, lanes):
                 piece = found[:, k : k + lanes]
@@ -301,7 +343,7 @@
             for k in range(0, chunk, lanes):
                 piece = weight[:, k : k + lanes]
                 total = piece if total is None else total + piece
-            product = mm(weight.astype(bf16), key_ref[begin : begin + chunk, :latent])
+            product = mm(weight.astype(bf16), key_block(begin, slice(0, latent)))
             summed = product if summed is None else summed + product
         shrink = jnp.exp2((stat_ref[at, :1] - top) * scale)
         total = jnp.sum(total, axis=1, keepdims=True) + shrink * stat_ref[at, 64:65]
@@ -320,9 +362,9 @@
         decode_ref[k] = jnp.where(hit, arrive_ref[...], cache_ref[k].astype(f32)).astype(bf16)
 
 
-def attend(length, dest, queries, own, peer, acc, stat, cache, pages, block=1024, sub=256, chunk=256):
-    count, width = queries.shape
-    latent = 4 * lanes
+def attend(length, dest, queries, ropes, own, mine, peer, acc, stat, cache, pages, block=1024, sub=256, chunk=256):
+    count, latent = queries.shape
+    width = latent + lanes
     keys = 64 * pages
     steps = count // block
     whole = lambda a: pl.BlockSpec(a.shape, lambda i: (0,) * a.ndim)
@@ -332,23 +374,23 @@
     return pl.pallas_call(
         functools.partial(attend_kernel, pages, sub, chunk),
         grid=(steps,),
-        in_specs=[scalar, scalar, strip(width), whole(own), whole(peer), strip(latent), strip(lanes), share],
+        in_specs=[scalar, scalar, strip(latent), strip(lanes), whole(own), whole(mine), whole(peer), strip(latent), strip(lanes), share],
         out_specs=[strip(latent), share],
         out_shape=[
             jax.ShapeDtypeStruct((count, latent), bf16),
             jax.ShapeDtypeStruct(cache.shape, bf16),
         ],
         scratch_shapes=[
-            pltpu.VMEM((keys, width), bf16),
+            pltpu.VMEM((keys // 2, width), bf16),
             pltpu.VMEM((2, sub, keys), f32),
             pltpu.VMEM(cache.shape[1:], f32),
-            pltpu.VMEM(own.shape, f32),
+            pltpu.VMEM(peer.shape, f32),
         ],
         compiler_params=pltpu.CompilerParams(vmem_limit_bytes=48 * 1024 * 1024),
         cost_estimate=pl.CostEstimate(
             flops=2 * count * keys * (width + latent), bytes_accessed=20_000_000, transcendentals=count * keys
         ),
-    )(length, dest, queries, own, peer, acc, stat, cache)
+    )(length, dest, queries, ropes, own, mine, peer, acc, stat, cache)
 
 
 def body(
@@ -373,16 +415,18 @@
     mark = jnp.broadcast_to(
         (token[:, None] == token[None, :]).astype(bf16)[:, None, :], (stretch, heads, stretch)
     )
-    queries = jnp.concatenate([q_latent, q_rope.reshape(stretch, heads, rope), mark], axis=2)
-    queries = queries.reshape(stretch * heads, latent + rope + stretch)
-    acc, stat = attend_fresh(queries, new_latent)
+    ropes = jnp.concatenate([q_rope.reshape(stretch, heads, rope), mark], axis=2)
+    ropes = ropes.reshape(stretch * heads, lanes)
+    queries = q_latent.reshape(stretch * heads, latent)
+    acc, stat = attend_fresh(queries, ropes, new_latent)
     held, acc, stat = lax.optimization_barrier((held, acc, stat))
 
     pages = page_owner.shape[1]
     own = lax.all_to_all(collect(held, pages), "pool", split_axis=0, concat_axis=0, tiled=True)
     own = own.reshape(-1, lanes)
     peer = lax.ppermute(own, "pd", [(0, 1), (1, 0)])
-    context, decode_out = attend(prefix_len, dest_slot, queries, own, peer, acc, stat, decode_cache, pages)
+    own, mine = unpack_own(prefix_len, own, pages, new_latent.shape[1])
+    context, decode_out = attend(prefix_len, dest_slot, queries, ropes, own, mine, peer, acc, stat, decode_cache, pages)
     return (context.reshape(stretch, heads, latent), decode_out)
 
 

time: 110 us -> 108 us (0.982)
  other arithmetic: 4.29 us -> 0.59 us
  waiting for transfers between devices: 3.43 us -> 6.92 us
  blocking collectives: 35.8 us -> 33 us
    all_to_all x1, waiting for transfers between devices: 2.53 us -> 6.54 us  [body(): lax.all_to_all(outgoing, 'pool', split_axis=0, concat_axis=0, tiled=True)]
    concatenate x1, other arithmetic: 4.28 us -> 0.58 us  [body(): jnp.concatenate([q_rope.reshape(stretch, heads, rope), mark], axis=2)]
    all_to_all x1, blocking collectives: 35.8 us -> 33 us  [body(): lax.all_to_all(collect(held, pages), 'pool', split_axis=0, concat_axis=0,...]
    unnamed x8 -> x12, local copies, waits for them, and re-layouts: 2.39 us -> 2.78 us
  transfers between devices with their start and end apart: 2 -> 2, of which waited for: 2 -> 2; matrix products, arithmetic and copies ran while one was open for 5% -> 2% of each run, Pallas kernels for 8% -> 8%
where the time goes in v4:
time: 108 us; the launch traced here: 107 us
  Pallas kernels  38.6 us (36%)
  blocking collectives  33 us (31%)
  starting transfers between devices  21.5 us (20%)
  waiting for transfers between devices  6.92 us (6%)
  local copies, waits for them, and re-layouts  4.04 us (4%)
  between operations  2.67 us (2%)
    all_to_all x1, blocking collectives, body(): lax.all_to_all(collect(held, pages), 'pool', split_axis=0, concat_axis=0,...  33 us
    pallas_call x1, Pallas kernels, attend(): pl.pallas_call(functools.partial(attend_kernel, pages, sub, chunk), grid=...  22.7 us
    all_to_all x1, starting transfers between devices, body(): lax.all_to_all(outgoing, 'pool', split_axis=0, concat_axis=0, tiled=True)  16.3 us
    pallas_call x1, Pallas kernels, attend_fresh(): pl.pallas_call(functools.partial(fresh_kernel, sub), grid=(count // block...  7.82 us
    all_to_all x1, waiting for transfers between devices, body(): lax.all_to_all(outgoing, 'pool', split_axis=0, concat_axis=0, tiled=True)  6.54 us
    ppermute x1, starting transfers between devices, body(): peer = lax.ppermute(own, 'pd', [(0, 1), (1, 0)])  5.17 us
    pallas_call x1, Pallas kernels, collect(): pl.pallas_call(functools.partial(collect_kernel, pages, 4), in_specs=[pl....  3.79 us
    pallas_call x1, Pallas kernels, spread(): pl.pallas_call(spread_kernel, grid=(2,), in_specs=[pl.BlockSpec(memory_sp...  3.75 us
  transfers between devices with their start and end apart: 2, of which 2 were waited for; matrix products, arithmetic and copies ran while one was open for 2% of the time, Pallas kernels for 8%

profile of v4, /device:TPU:1, one launch (start us, length us, event | category | flops | bytes accessed | tf_op | source)
XLA Modules:
  0.0 107.4 jit_solution(14545447990111690628)
XLA Ops:
  1.3 0.0 copy-start.5
  1.3 3.8 %shard_map.113 = bf16[2560,128]{1,0:T(8,128)(2,1)} custom-call(s32[1]{0:T(128)S(6)} %copy.13.partner_ref, bf16[16,2,2,16,576]{4,3,2,1,0:T(8,128)(2,1)} %bitcast.18, bf16[2,2,16,576]{3,2,1,0:T(8,128)(2,1)} %bitcast.15, s32[1,24]{1,0:T(1,128)} %owner_ref.1, s32[1,24]{1,0:T(1,128)} %slot_ref.1), custom_call_target="tpu_custom_call" | custom-call | flops 1000000000 | bytes 1500000 | tf_op jit(solution)/shard_map/pallas_call | solution.py:89
  5.0 16.3 %all-to-all-start = ((bf16[128,10,2,128]{3,2,1,0:T(2,128)(2,1)}), bf16[128,10,2,128]{3,2,1,0:T(2,128)(2,1)S(1)}, u32[]{:S(2)}, u32[]{:S(2)}) async-start(bf16[128,10,2,128]{3,2,1,0:T(2,128)(2,1)} %bitcast.17), calls=%async_computation | async-start | bytes 1310720 | tf_op jit(solution)/shard_map/all_to_all | solution.py:412
  21.4 0.0 copy-done.5
  21.4 0.0 copy-start.2
  21.4 1.1 %concatenate.8 = bf16[4096,64]{1,0:T(8,128)(2,1)S(1)} reshape(bf16[64,4096]{1,0:T(8,128)(2,1)S(1)} %copy-done.5) | data formatting | bytes 1048576 | tf_op jit(solution)/shard_map/concatenate | solution.py:418
  22.6 0.0 copy-start
  22.6 0.1 broadcast_in_dim.2
  22.7 0.6 pad_maximum_fusion.rope_ref
  23.3 0.0 copy-done.2
  23.3 1.4 %copy-done = bf16[64,64,512]{2,1,0:T(8,128)(2,1)S(1)} copy-done((bf16[64,64,512]{2,1,0:T(8,128)(2,1)S(1)}, bf16[64,64,512]{2,1,0:T(8,128)(2,1)}, u32[]{:S(2)}) %copy-start) | copy-done | bytes 4194328
  24.7 7.8 %shard_map.114 = (f32[4096,512]{1,0:T(8,128)}, f32[4096,128]{1,0:T(8,128)S(1)}) custom-call(bf16[4096,512]{1,0:T(8,128)(2,1)S(1)} %bitcast.14, bf16[4096,128]{1,0:T(8,128)(2,1)S(1)} %pad_maximum_fusion.rope_ref, bf16[64,576]{1,0:T(8,128)(2,1)S(1)} %copy-done.2), custom_call_target="tpu_custom_call" | custom-call | flops 5000000000 | bytes 16000000 | tf_op jit(solution)/shard_map/pallas_call | solution.py:206
  32.6 0.0 copy-start.3
  32.6 1.3 %copy-done.3 = f32[4096,128]{1,0:T(8,128)} copy-done((f32[4096,128]{1,0:T(8,128)}, f32[4096,128]{1,0:T(8,128)S(1)}, u32[]{:S(2)}) %copy-start.3) | copy-done | bytes 2097176
  33.9 6.5 %all-to-all-done = bf16[128,10,2,128]{3,2,1,0:T(2,128)(2,1)S(1)} async-done(((bf16[128,10,2,128]{3,2,1,0:T(2,128)(2,1)}), bf16[128,10,2,128]{3,2,1,0:T(2,128)(2,1)S(1)}, u32[]{:S(2)}, u32[]{:S(2)}) %all-to-all-start) | async-done | bytes 655392 | tf_op jit(solution)/shard_map/all_to_all | solution.py:412
  40.4 3.8 %shard_map.115 = bf16[3840,128]{1,0:T(8,128)(2,1)S(1)} custom-call(bf16[2560,128]{1,0:T(8,128)(2,1)S(1)} %bitcast.12), custom_call_target="tpu_custom_call" | custom-call | flops 4000000000 | bytes 1500000 | tf_op jit(solution)/shard_map/pallas_call | solution.py:155
  44.2 33.0 %all_to_all.10 = bf16[128,15,2,128]{3,2,1,0:T(2,128)(2,1)S(1)} all-to-all(bf16[128,15,2,128]{3,2,1,0:T(2,128)(2,1)S(1)} %bitcast.11), channel_id=1, replica_groups=mesh['pool'=128,'pd'=2] {'pool'}, dimensions={0} | all-to-all | bytes 1966080 | tf_op jit(solution)/shard_map/all_to_all | solution.py:425
  77.3 0.0 copy-start.1
  77.3 0.0 copy-start.4
  77.3 5.2 %collective-permute-start = (bf16[3840,128]{1,0:T(8,128)(2,1)S(1)}, bf16[3840,128]{1,0:T(8,128)(2,1)S(1)}, u32[]{:S(2)}, u32[]{:S(2)}) collective-permute-start(bf16[3840,128]{1,0:T(8,128)(2,1)S(1)} %bitcast.9), channel_id=1, source_target_pairs={{0,1},{1,0},{2,3},{3,2},{4,5},{5,4},{6,7},{7,6},{8,9},{9,8},{10,11... | collective-permute-start | bytes 2949128 | tf_op jit(solution)/shard_map/ppermute | solution.py:427
  83.7 0.5 shard_map.116
  84.3 0.4 collective-permute-done.peer_ref
  84.6 0.0 copy-done.1
  84.6 0.0 copy-done.4
  84.6 22.7 %shard_map.117 = (bf16[4096,512]{1,0:T(8,128)(2,1)}, bf16[8,64,576]{2,1,0:T(8,128)(2,1)}) custom-call(s32[1]{0:T(128)S(6)} %copy.12.length_ref, s32[1]{0:T(128)S(6)} %copy.14.dest_ref, bf16[4096,512]{1,0:T(8,128)(2,1)} %bitcast.13, bf16[4096,128]{1,0:T(8,128)(2,1)S(1)} %pad_maximum_fusion.rope_ref, bf16[768,640]{1,0:T(8,128)(2,1)S(1)} %get-tuple-element.14.own_ref, ...), custom_call_target="tpu_custom_call" | custom-call | flops 14495514624 | bytes 20000000 | tf_op jit(solution)/shard_map/pallas_call | solution.py:374
  (1 shorter events, 0.0 us)
Async XLA Ops:
  1.3 20.1 %copy-start.5 = (bf16[64,4096]{1,0:T(8,128)(2,1)S(1)}, bf16[64,4096]{1,0:T(8,128)(2,1)}, u32[]{:S(2)}) copy-start(bf16[64,4096]{1,0:T(8,128)(2,1)} %param.11) | copy-start | bytes 1572868
  5.0 35.4 %all-to-all-start = ((bf16[128,10,2,128]{3,2,1,0:T(2,128)(2,1)}), bf16[128,10,2,128]{3,2,1,0:T(2,128)(2,1)S(1)}, u32[]{:S(2)}, u32[]{:S(2)}) async-start(bf16[128,10,2,128]{3,2,1,0:T(2,128)(2,1)} %bitcast.17), calls=%async_computation | async-start | bytes 1310720 | tf_op jit(solution)/shard_map/all_to_all | solution.py:412
  21.4 1.9 %copy-start.2 = (bf16[64,576]{1,0:T(8,128)(2,1)S(1)}, bf16[64,576]{1,0:T(8,128)(2,1)}, u32[]{:S(2)}) copy-start(bf16[64,576]{1,0:T(8,128)(2,1)} %new_ref.1) | copy-start | bytes 221188
  22.6 2.2 %copy-start = (bf16[64,64,512]{2,1,0:T(8,128)(2,1)S(1)}, bf16[64,64,512]{2,1,0:T(8,128)(2,1)}, u32[]{:S(2)}) copy-start(bf16[64,64,512]{2,1,0:T(8,128)(2,1)} %param.10) | copy-start | bytes 12582916
  32.6 1.3 %copy-start.3 = (f32[4096,128]{1,0:T(8,128)}, f32[4096,128]{1,0:T(8,128)S(1)}, u32[]{:S(2)}) copy-start(f32[4096,128]{1,0:T(8,128)S(1)} %get-tuple-element.17.stat_ref) | copy-start | bytes 6291460
  77.3 7.4 %copy-start.1 = (bf16[8,64,576]{2,1,0:T(8,128)(2,1)S(1)}, bf16[8,64,576]{2,1,0:T(8,128)(2,1)}, u32[]{:S(2)}) copy-start(bf16[8,64,576]{2,1,0:T(8,128)(2,1)} %cache_ref.1) | copy-start | bytes 1769476
  77.3 7.4 %copy-start.4 = (f32[4096,128]{1,0:T(8,128)S(1)}, f32[4096,128]{1,0:T(8,128)}, u32[]{:S(2)}) copy-start(f32[4096,128]{1,0:T(8,128)} %copy-done.3) | copy-start | bytes 6291460
  77.3 7.4 %collective-permute-start = (bf16[3840,128]{1,0:T(8,128)(2,1)S(1)}, bf16[3840,128]{1,0:T(8,128)(2,1)S(1)}, u32[]{:S(2)}, u32[]{:S(2)}) collective-permute-start(bf16[3840,128]{1,0:T(8,128)(2,1)S(1)} %bitcast.9), channel_id=1, source_target_pairs={{0,1},{1,0},{2,3},{3,2},{4,5},{5,4},{6,7},{7,6},{8,9},{9,8},{10,11... | collective-permute-start | bytes 2949128 | tf_op jit(solution)/shard_map/ppermute | solution.py:427

commit v5 on v4

--- a/solution.py
+++ b/solution.py
@@ -123,20 +123,22 @@
     meta = rows_ref[pl.ds(19, owners, stride=held), :]
     blank = jnp.zeros((owners, lanes), f32)
     ropes = [blank] * (pages // 8)
-    for start in range(0, pages, group):
+    for start in range(pages - group, -1, -group):
         wanted = []
-        for place in range(start, start + group):
+        for place in range(start + group - 1, start - 1, -1):
             owner = picks(meta[:, 32 + place : 33 + place] == lane.astype(f32))
             slot = jnp.broadcast_to(meta[:, 64 + place : 65 + place], (owners, lanes)).astype(bf16)
-            wanted.append(
-                jnp.concatenate(
-                    [jnp.where(slot == jnp.bfloat16(k), owner, jnp.bfloat16(0)) for k in range(slots)], axis=1
-                )
+            one = jnp.concatenate(
+                [jnp.where(slot == jnp.bfloat16(k), owner, jnp.bfloat16(0)) for k in range(slots)], axis=1
             )
+            wanted.append(one if place > 0 else one[:16])
         found = mm(jnp.concatenate(wanted, axis=0), table_ref[...])
         for k in range(group):
-            place = start + k
-            got = found[k * owners : (k + 1) * owners]
+            place = start + group - 1 - k
+            if place > 0:
+                got = found[k * owners : (k + 1) * owners]
+            else:
+                got = jnp.broadcast_to(found[k * owners : k * owners + 1], (owners, 2 * lanes))
             stage_ref[pl.ds(place, owners, stride=size), :] = got[:, :lanes]
             ropes[place // 8] += jnp.where((lane >> 4) == place % 8, got[:, lanes:], 0.0)
     comes = picks(meta[:, 96:97].astype(jnp.int32) == lane)

time: 108 us -> 108 us (level)
  no operation moved by 1% of the time
where the time goes in v5:
time: 108 us; the launch traced here: 107 us
  Pallas kernels  38.5 us (36%)
  blocking collectives  33 us (31%)
  starting transfers between devices  21.5 us (20%)
  waiting for transfers between devices  6.92 us (6%)
  local copies, waits for them, and re-layouts  4.04 us (4%)
  between operations  2.67 us (2%)
    all_to_all x1, blocking collectives, body(): lax.all_to_all(collect(held, pages), 'pool', split_axis=0, concat_axis=0,...  33 us
    pallas_call x1, Pallas kernels, attend(): pl.pallas_call(functools.partial(attend_kernel, pages, sub, chunk), grid=...  22.7 us
    all_to_all x1, starting transfers between devices, body(): lax.all_to_all(outgoing, 'pool', split_axis=0, concat_axis=0, tiled=True)  16.3 us
    pallas_call x1, Pallas kernels, attend_fresh(): pl.pallas_call(functools.partial(fresh_kernel, sub), grid=(count // block...  7.82 us
    all_to_all x1, waiting for transfers between devices, body(): lax.all_to_all(outgoing, 'pool', split_axis=0, concat_axis=0, tiled=True)  6.54 us
    ppermute x1, starting transfers between devices, body(): peer = lax.ppermute(own, 'pd', [(0, 1), (1, 0)])  5.18 us
    pallas_call x1, Pallas kernels, spread(): pl.pallas_call(spread_kernel, grid=(2,), in_specs=[pl.BlockSpec(memory_sp...  3.75 us
    pallas_call x1, Pallas kernels, collect(): pl.pallas_call(functools.partial(collect_kernel, pages, 4), in_specs=[pl....  3.69 us
  transfers between devices with their start and end apart: 2, of which 2 were waited for; matrix products, arithmetic and copies ran while one was open for 2% of the time, Pallas kernels for 8%

profile of v5, /device:TPU:1, one launch (start us, length us, event | category | flops | bytes accessed | tf_op | source)
XLA Modules:
  0.0 107.3 jit_solution(11478249633959071844)
XLA Ops:
  1.3 0.0 copy-start.5
  1.3 3.8 %shard_map.113 = bf16[2560,128]{1,0:T(8,128)(2,1)} custom-call(s32[1]{0:T(128)S(6)} %copy.13.partner_ref, bf16[16,2,2,16,576]{4,3,2,1,0:T(8,128)(2,1)} %bitcast.18, bf16[2,2,16,576]{3,2,1,0:T(8,128)(2,1)} %bitcast.15, s32[1,24]{1,0:T(1,128)} %owner_ref.1, s32[1,24]{1,0:T(1,128)} %slot_ref.1), custom_call_target="tpu_custom_call" | custom-call | flops 1000000000 | bytes 1500000 | tf_op jit(solution)/shard_map/pallas_call | solution.py:89
  5.0 16.3 %all-to-all-start = ((bf16[128,10,2,128]{3,2,1,0:T(2,128)(2,1)}), bf16[128,10,2,128]{3,2,1,0:T(2,128)(2,1)S(1)}, u32[]{:S(2)}, u32[]{:S(2)}) async-start(bf16[128,10,2,128]{3,2,1,0:T(2,128)(2,1)} %bitcast.17), calls=%async_computation | async-start | bytes 1310720 | tf_op jit(solution)/shard_map/all_to_all | solution.py:414
  21.4 0.0 copy-done.5
  21.4 0.0 copy-start.2
  21.4 1.1 %concatenate.8 = bf16[4096,64]{1,0:T(8,128)(2,1)S(1)} reshape(bf16[64,4096]{1,0:T(8,128)(2,1)S(1)} %copy-done.5) | data formatting | bytes 1048576 | tf_op jit(solution)/shard_map/concatenate | solution.py:420
  22.6 0.0 copy-start
  22.6 0.1 broadcast_in_dim.2
  22.7 0.6 pad_maximum_fusion.rope_ref
  23.3 0.0 copy-done.2
  23.3 1.4 %copy-done = bf16[64,64,512]{2,1,0:T(8,128)(2,1)S(1)} copy-done((bf16[64,64,512]{2,1,0:T(8,128)(2,1)S(1)}, bf16[64,64,512]{2,1,0:T(8,128)(2,1)}, u32[]{:S(2)}) %copy-start) | copy-done | bytes 4194328
  24.7 7.8 %shard_map.114 = (f32[4096,512]{1,0:T(8,128)}, f32[4096,128]{1,0:T(8,128)S(1)}) custom-call(bf16[4096,512]{1,0:T(8,128)(2,1)S(1)} %bitcast.14, bf16[4096,128]{1,0:T(8,128)(2,1)S(1)} %pad_maximum_fusion.rope_ref, bf16[64,576]{1,0:T(8,128)(2,1)S(1)} %copy-done.2), custom_call_target="tpu_custom_call" | custom-call | flops 5000000000 | bytes 16000000 | tf_op jit(solution)/shard_map/pallas_call | solution.py:208
  32.6 0.0 copy-start.3
  32.6 1.3 %copy-done.3 = f32[4096,128]{1,0:T(8,128)} copy-done((f32[4096,128]{1,0:T(8,128)}, f32[4096,128]{1,0:T(8,128)S(1)}, u32[]{:S(2)}) %copy-start.3) | copy-done | bytes 2097176
  33.9 6.5 %all-to-all-done = bf16[128,10,2,128]{3,2,1,0:T(2,128)(2,1)S(1)} async-done(((bf16[128,10,2,128]{3,2,1,0:T(2,128)(2,1)}), bf16[128,10,2,128]{3,2,1,0:T(2,128)(2,1)S(1)}, u32[]{:S(2)}, u32[]{:S(2)}) %all-to-all-start) | async-done | bytes 655392 | tf_op jit(solution)/shard_map/all_to_all | solution.py:414
  40.4 3.7 %shard_map.115 = bf16[3840,128]{1,0:T(8,128)(2,1)S(1)} custom-call(bf16[2560,128]{1,0:T(8,128)(2,1)S(1)} %bitcast.12), custom_call_target="tpu_custom_call" | custom-call | flops 4000000000 | bytes 1500000 | tf_op jit(solution)/shard_map/pallas_call | solution.py:157
  44.1 33.0 %all_to_all.10 = bf16[128,15,2,128]{3,2,1,0:T(2,128)(2,1)S(1)} all-to-all(bf16[128,15,2,128]{3,2,1,0:T(2,128)(2,1)S(1)} %bitcast.11), channel_id=1, replica_groups=mesh['pool'=128,'pd'=2] {'pool'}, dimensions={0} | all-to-all | bytes 1966080 | tf_op jit(solution)/shard_map/all_to_all | solution.py:427
  77.2 0.0 copy-start.1
  77.2 0.0 copy-start.4
  77.2 5.2 %collective-permute-start = (bf16[3840,128]{1,0:T(8,128)(2,1)S(1)}, bf16[3840,128]{1,0:T(8,128)(2,1)S(1)}, u32[]{:S(2)}, u32[]{:S(2)}) collective-permute-start(bf16[3840,128]{1,0:T(8,128)(2,1)S(1)} %bitcast.9), channel_id=1, source_target_pairs={{0,1},{1,0},{2,3},{3,2},{4,5},{5,4},{6,7},{7,6},{8,9},{9,8},{10,11... | collective-permute-start | bytes 2949128 | tf_op jit(solution)/shard_map/ppermute | solution.py:429
  83.7 0.5 shard_map.116
  84.2 0.4 collective-permute-done.peer_ref
  84.6 0.0 copy-done.1
  84.6 0.0 copy-done.4
  84.6 22.7 %shard_map.117 = (bf16[4096,512]{1,0:T(8,128)(2,1)}, bf16[8,64,576]{2,1,0:T(8,128)(2,1)}) custom-call(s32[1]{0:T(128)S(6)} %copy.12.length_ref, s32[1]{0:T(128)S(6)} %copy.14.dest_ref, bf16[4096,512]{1,0:T(8,128)(2,1)} %bitcast.13, bf16[4096,128]{1,0:T(8,128)(2,1)S(1)} %pad_maximum_fusion.rope_ref, bf16[768,640]{1,0:T(8,128)(2,1)S(1)} %get-tuple-element.14.own_ref, ...), custom_call_target="tpu_custom_call" | custom-call | flops 14495514624 | bytes 20000000 | tf_op jit(solution)/shard_map/pallas_call | solution.py:376
  (1 shorter events, 0.0 us)
Async XLA Ops:
  1.3 20.1 %copy-start.5 = (bf16[64,4096]{1,0:T(8,128)(2,1)S(1)}, bf16[64,4096]{1,0:T(8,128)(2,1)}, u32[]{:S(2)}) copy-start(bf16[64,4096]{1,0:T(8,128)(2,1)} %param.11) | copy-start | bytes 1572868
  5.0 35.4 %all-to-all-start = ((bf16[128,10,2,128]{3,2,1,0:T(2,128)(2,1)}), bf16[128,10,2,128]{3,2,1,0:T(2,128)(2,1)S(1)}, u32[]{:S(2)}, u32[]{:S(2)}) async-start(bf16[128,10,2,128]{3,2,1,0:T(2,128)(2,1)} %bitcast.17), calls=%async_computation | async-start | bytes 1310720 | tf_op jit(solution)/shard_map/all_to_all | solution.py:414
  21.4 1.9 %copy-start.2 = (bf16[64,576]{1,0:T(8,128)(2,1)S(1)}, bf16[64,576]{1,0:T(8,128)(2,1)}, u32[]{:S(2)}) copy-start(bf16[64,576]{1,0:T(8,128)(2,1)} %new_ref.1) | copy-start | bytes 221188
  22.6 2.2 %copy-start = (bf16[64,64,512]{2,1,0:T(8,128)(2,1)S(1)}, bf16[64,64,512]{2,1,0:T(8,128)(2,1)}, u32[]{:S(2)}) copy-start(bf16[64,64,512]{2,1,0:T(8,128)(2,1)} %param.10) | copy-start | bytes 12582916
  32.6 1.3 %copy-start.3 = (f32[4096,128]{1,0:T(8,128)}, f32[4096,128]{1,0:T(8,128)S(1)}, u32[]{:S(2)}) copy-start(f32[4096,128]{1,0:T(8,128)S(1)} %get-tuple-element.17.stat_ref) | copy-start | bytes 6291460
  77.2 7.4 %copy-start.1 = (bf16[8,64,576]{2,1,0:T(8,128)(2,1)S(1)}, bf16[8,64,576]{2,1,0:T(8,128)(2,1)}, u32[]{:S(2)}) copy-start(bf16[8,64,576]{2,1,0:T(8,128)(2,1)} %cache_ref.1) | copy-start | bytes 1769476
  77.2 7.4 %copy-start.4 = (f32[4096,128]{1,0:T(8,128)S(1)}, f32[4096,128]{1,0:T(8,128)}, u32[]{:S(2)}) copy-start(f32[4096,128]{1,0:T(8,128)} %copy-done.3) | copy-start | bytes 6291460
  77.2 7.4 %collective-permute-start = (bf16[3840,128]{1,0:T(8,128)(2,1)S(1)}, bf16[3840,128]{1,0:T(8,128)(2,1)S(1)}, u32[]{:S(2)}, u32[]{:S(2)}) collective-permute-start(bf16[3840,128]{1,0:T(8,128)(2,1)S(1)} %bitcast.9), channel_id=1, source_target_pairs={{0,1},{1,0},{2,3},{3,2},{4,5},{5,4},{6,7},{7,6},{8,9},{9,8},{10,11... | collective-permute-start | bytes 2949128 | tf_op jit(solution)/shard_map/ppermute | solution.py:429
